TPU v7x, 512 devices: a whole 4x8x8 slice. The times are simulated.
512 devices in a mesh: band: 16 (over x_lo, y), fft: 32 (over z, x_hi, core).
Axes of the slice: x: 4 (x_hi: 2, x_lo: 2; x = x_hi * 2 + x_lo), y: 8, z: 8, core: 2. Of those that a mesh axis runs over, the one named last changes fastest.
Arguments:
- orbitals: float32 [32, 128, 128, 128], P('band', 'fft'), may hold values from -2 to 2
- owner: int32 [4], replicated, may hold values from 0 to 15
- occupied: int32 [16, 2], replicated, may hold values from 0 to 1, as said below
Outputs:
- exchange: float32 [32, 128, 128, 128], P('band', 'fft')
Inputs may be any that keep to these rules, and one draw needn't show every extreme that they name: `occupied`: each row names 2 different local orbitals of its band group.
All inputs are finite; a program needn't handle non-finite values.
Results may differ from a plain program's by a relative error of at most 0.0001.
Values sent between devices are 32-bit elements; how exact they have to be, the bound alone decides.
No kernel may reach another device: no remote copies, remote signals or barrier semaphores. Data moves between devices by JAX's collectives and lax.ppermute only.
A program may use at most 64 MiB of HBM per device.

v0:
```python
import math

import jax
import jax.numpy as jnp
import numpy as np
from jax import lax
from jax.experimental import pallas as pl
from jax.experimental.pallas import tpu as pltpu
from jax.sharding import PartitionSpec as P

SCREEN = 0.025
FRACTION = 0.25
LANES = 128
VMEM_LIMIT = 40 * 1024 * 1024


def wave_matrix(length):
    indices = np.arange(length)
    angles = (indices[:, None] * indices[None, :] % length) * (2.0 * math.pi / length)
    cosine, sine = np.cos(angles), np.sin(angles)
    return np.block([[cosine, sine], [-sine, cosine]]).astype(np.float32)


def split(value):
    high = value.astype(jnp.bfloat16)
    low = (value - high.astype(jnp.float32)).astype(jnp.bfloat16)
    return high, low


def dot(left, right):
    return jnp.dot(left, right, preferred_element_type=jnp.float32)


def left_product(matrix, value):
    high, low = split(value)
    return dot(matrix[0], high) + (dot(matrix[0], low) + dot(matrix[1], high))


def right_product(value, matrix):
    high, low = split(value)
    return dot(high, matrix[0]) + (dot(low, matrix[0]) + dot(high, matrix[1]))


def forward_kernel(order, orbitals, received, left, right, out):
    planes, length = orbitals.shape[1], orbitals.shape[2]
    partners = received.shape[0]
    stride = partners * 2 * planes
    left, right = split(left[...]), split(right[...])
    for j in range(partners):
        for p in range(planes):
            partner = received[order[j], p]
            field = jnp.concatenate([orbitals[0, p] * partner, orbitals[1, p] * partner], axis=1)
            along_z = right_product(field, right)
            stacked = jnp.concatenate([along_z[:, :length], along_z[:, length:]], axis=0)
            both = left_product(left, stacked)
            for c in range(2):
                row = (j * 2 + c) * planes + p
                out[pl.ds(row, length, stride=stride), :] = both[c * length : (c + 1) * length]


def signed_wave(index, length):
    signed = jnp.where(index <= length // 2, index, index - length)
    return signed.astype(jnp.float32) * (2.0 * math.pi / length)


def middle_kernel(first, field, forward, backward, out):
    sources, rows, partners, parts, lanes = field.shape
    planes = parts // 2
    length = sources * planes
    size = sources * parts
    row = lax.broadcasted_iota(jnp.int32, (size, lanes), 0)
    x_index = (row // parts) * planes + row % planes
    wave_x = signed_wave(x_index, length)
    wave_z = signed_wave(lax.broadcasted_iota(jnp.int32, (size, lanes), 1), length)
    flat = wave_x * wave_x + wave_z * wave_z + SCREEN
    forward, backward = split(forward[...]), split(backward[...])
    factor = -FRACTION * 4.0 * math.pi / float(length**3)
    for k in range(rows):
        wave_y = signed_wave(first[0] + k, length)
        kernel = factor / (flat + wave_y * wave_y)
        for j in range(partners):
            value = field[:, k, j].reshape(size, lanes)
            value = left_product(forward, value) * kernel
            value = left_product(backward, value)
            out[:, k, j] = value.reshape(sources, parts, lanes)


def backward_kernel(order, field, received, left, right, out):
    planes, length = received.shape[1], received.shape[2]
    partners = received.shape[0]
    stride = partners * 2 * planes
    left, right = split(left[...]), split(right[...])
    for p in range(planes):
        totals = None
        for j in range(partners):
            partner = received[order[j], p]
            stacked = jnp.concatenate(
                [field[pl.ds((j * 2 + c) * planes + p, length, stride=stride), :] for c in range(2)],
                axis=0,
            )
            along_y = left_product(left, stacked)
            wide = jnp.concatenate([along_y[:length], along_y[length:]], axis=1)
            both = right_product(wide, right)
            terms = [both[:, :length] * partner, both[:, length:] * partner]
            totals = terms if totals is None else [a + b for a, b in zip(totals, terms)]
        for c in range(2):
            out[c, p] = totals[c]


def smem():
    return pl.BlockSpec(memory_space=pltpu.SMEM)


def vmem():
    return pl.BlockSpec(memory_space=pltpu.VMEM)


def call(kernel, shape, specs, flops, name):
    return pl.pallas_call(
        kernel,
        out_shape=jax.ShapeDtypeStruct(shape, jnp.float32),
        in_specs=specs,
        out_specs=vmem(),
        compiler_params=pltpu.CompilerParams(vmem_limit_bytes=VMEM_LIMIT),
        cost_estimate=pl.CostEstimate(flops=flops, bytes_accessed=4 << 20, transcendentals=0),
        name=name,
    )


def body(orbitals, owner, occupied):
    bands, planes, length, _ = orbitals.shape
    groups = lax.axis_size("band")
    columns = lax.axis_size("fft")
    rows = length // columns
    partners = occupied.shape[1]
    leader = owner[0]
    order = lax.dynamic_index_in_dim(occupied, leader, 0, keepdims=False)

    pieces = orbitals.reshape(groups, -1, LANES)
    with jax.named_scope("scatter"):
        pieces = lax.all_to_all(pieces, "band", 0, 0, tiled=True)
        mine = lax.dynamic_index_in_dim(pieces, leader, 0, keepdims=True)
        mine = jnp.broadcast_to(mine, pieces.shape)
    with jax.named_scope("gather"):
        received = lax.all_to_all(mine, "band", 0, 0, tiled=True).reshape(orbitals.shape)

    matrix = wave_matrix(length)
    left, right = matrix, matrix.T.copy()
    x_index = np.arange(length).reshape(columns, 1, planes) + np.array([0, length])[None, :, None]
    x_index = x_index.reshape(-1)
    mixed = matrix[np.ix_(x_index, x_index)]
    x_forward, x_backward = mixed, mixed.T.copy()

    size = 3 * 2 * 2 * length * 2 * length * partners * planes * length * 2
    total = length * partners * 2 * planes
    spectrum = call(
        forward_kernel, (total, LANES), [smem()] + [vmem()] * 4, size, "forward_zy"
    )(order, orbitals, received, left, right)
    with jax.named_scope("to_columns"):
        spectrum = lax.all_to_all(
            spectrum.reshape(columns, rows * partners * 2 * planes, LANES), "fft", 0, 0, tiled=True
        )
    first = (lax.axis_index("fft") * rows).astype(jnp.int32).reshape(1)
    shape = (columns, rows, partners, 2 * planes, LANES)
    spectrum = call(
        middle_kernel, shape, [smem()] + [vmem()] * 3, size, "solve_x"
    )(first, spectrum.reshape(shape), x_forward, x_backward)
    with jax.named_scope("to_planes"):
        spectrum = lax.all_to_all(
            spectrum.reshape(columns, rows * partners * 2 * planes, LANES), "fft", 0, 0, tiled=True
        )
    return call(
        backward_kernel, orbitals.shape, [smem()] + [vmem()] * 4, size, "backward_yz"
    )(order, spectrum.reshape(total, LANES), received, right, left)


def solution(mesh):
    return jax.shard_map(
        body,
        mesh=mesh,
        in_specs=(P("band", "fft", None, None), P(), P()),
        out_specs=P("band", "fft", None, None),
        check_vma=False,
    )
```

profile of v0, /device:TPU:1, one launch (start us, length us, event | category | flops | bytes accessed | tf_op | source)
XLA Modules:
  0.0 131.6 jit_solution(18302774536673662651)
XLA Ops:
  0.0 0.0 copy-start
  0.0 8.8 %all-to-all-start = ((f32[16,64,128]{2,1,0:T(8,128)}), f32[16,64,128]{2,1,0:T(8,128)S(1)}, u32[]{:S(2)}, u32[]{:S(2)}) async-start(f32[16,64,128]{2,1,0:T(8,128)} %bitcast.14), calls=%async_computation | async-start | bytes 1048576 | tf_op jit(solution)/shard_map/scatter/all_to_all | solution.py:141
  8.8 0.0 copy-start.6
  8.8 0.6 copy-done.6
  9.6 12.4 %all-to-all-done = f32[16,64,128]{2,1,0:T(8,128)S(1)} async-done(((f32[16,64,128]{2,1,0:T(8,128)}), f32[16,64,128]{2,1,0:T(8,128)S(1)}, u32[]{:S(2)}, u32[]{:S(2)}) %all-to-all-start) | async-done | bytes 524320 | tf_op jit(solution)/shard_map/scatter/all_to_all | solution.py:141
  22.0 0.8 broadcast_in_dim.8
  22.8 0.0 copy-start.1
  22.9 0.0 copy-start.2
  22.9 0.0 copy-start.3
  22.9 6.0 %all-to-all-start.1 = ((f32[16,64,128]{2,1,0:T(8,128)}), f32[16,64,128]{2,1,0:T(8,128)S(1)}, u32[]{:S(2)}, u32[]{:S(2)}) async-start(f32[16,64,128]{2,1,0:T(8,128)} %broadcast_in_dim.8), calls=%async_computation.1 | async-start | bytes 1048576 | tf_op jit(solution)/shard_map/gather/all_to_all | solution.py:145
  28.8 0.0 copy-done
  28.8 0.2 dynamic-slice_reduce_fusion.order
  29.0 12.6 %all-to-all-done.1 = f32[16,64,128]{2,1,0:T(8,128)S(1)} async-done(((f32[16,64,128]{2,1,0:T(8,128)}), f32[16,64,128]{2,1,0:T(8,128)S(1)}, u32[]{:S(2)}, u32[]{:S(2)}) %all-to-all-start.1) | async-done | bytes 524320 | tf_op jit(solution)/shard_map/gather/all_to_all | solution.py:145
  41.6 0.0 copy-done.1
  41.6 0.0 copy-done.2
  41.6 0.0 copy-done.3
  41.6 4.7 %forward_zy.1 = f32[2048,128]{1,0:T(8,128)} custom-call(s32[2]{0:T(128)S(1)} %dynamic-slice_reduce_fusion.order, f32[2,4,128,128]{3,2,1,0:T(8,128)S(1)} %copy-done.1, f32[2,4,128,128]{3,2,1,0:T(8,128)S(1)} %bitcast.15, f32[256,256]{1,0:T(8,128)S(1)} %copy-done.2, f32[256,256]{1,0:T(8,128)S(1)} %copy-done.3), custom_call_target="tpu_custom_call" | custom-call | flops 805306368 | bytes 4194304 | tf_op jit(solution)/shard_map/forward_zy/pallas_call | solution.py:156
  46.3 0.0 copy-start.4
  46.3 0.0 copy-start.5
  46.3 16.7 %all-to-all-start.2 = ((f32[32,64,128]{2,1,0:T(8,128)}), f32[32,64,128]{2,1,0:T(8,128)S(1)}, u32[]{:S(2)}, u32[]{:S(2)}) async-start(f32[32,64,128]{2,1,0:T(8,128)} %bitcast.5), calls=%async_computation.2 | async-start | bytes 2097152 | tf_op jit(solution)/shard_map/to_columns/all_to_all | solution.py:160
  63.0 28.1 %all-to-all-done.2 = f32[32,64,128]{2,1,0:T(8,128)S(1)} async-done(((f32[32,64,128]{2,1,0:T(8,128)}), f32[32,64,128]{2,1,0:T(8,128)S(1)}, u32[]{:S(2)}, u32[]{:S(2)}) %all-to-all-start.2) | async-done | bytes 1048608 | tf_op jit(solution)/shard_map/to_columns/all_to_all | solution.py:160
  91.2 0.0 copy-done.4
  91.2 0.0 copy-done.5
  91.2 3.0 %solve_x.1 = f32[32,4,2,8,128]{4,3,2,1,0:T(8,128)S(1)} custom-call(s32[1]{0:T(128)} %bitcast.1.first, f32[32,4,2,8,128]{4,3,2,1,0:T(8,128)S(1)} %bitcast.11, f32[256,256]{1,0:T(8,128)S(1)} %copy-done.4, f32[256,256]{1,0:T(8,128)S(1)} %copy-done.5), custom_call_target="tpu_custom_call" | custom-call | flops 805306368 | bytes 4194304 | tf_op jit(solution)/shard_map/solve_x/pallas_call | solution.py:165
  94.2 33.7 %all_to_all.20 = f32[32,64,128]{2,1,0:T(8,128)S(1)} all-to-all(f32[32,64,128]{2,1,0:T(8,128)S(1)} %bitcast.13), channel_id=1, replica_groups=mesh['band'=16,'fft'=32] {'fft'}, dimensions={0} | all-to-all | bytes 2097152 | tf_op jit(solution)/shard_map/to_planes/all_to_all | solution.py:169
  127.9 3.7 %backward_yz.1 = f32[2,4,128,128]{3,2,1,0:T(8,128)} custom-call(s32[2]{0:T(128)S(1)} %dynamic-slice_reduce_fusion.order, f32[2048,128]{1,0:T(8,128)S(1)} %bitcast.12, f32[2,4,128,128]{3,2,1,0:T(8,128)S(1)} %bitcast.16, f32[256,256]{1,0:T(8,128)S(1)} %copy-done.3, f32[256,256]{1,0:T(8,128)S(1)} %copy-done.2), custom_call_target="tpu_custom_call" | custom-call | flops 805306368 | bytes 4194304 | tf_op jit(solution)/shard_map/backward_yz/pallas_call | solution.py:172
  (1 shorter events, 0.0 us)
Async XLA Ops:
  0.0 28.8 %copy-start = (s32[16,2]{0,1:T(2,128)S(1)}, s32[16,2]{0,1:T(2,128)}, u32[]{:S(2)}) copy-start(s32[16,2]{0,1:T(2,128)} %param.9) | copy-start | bytes 388
  0.0 22.0 %all-to-all-start = ((f32[16,64,128]{2,1,0:T(8,128)}), f32[16,64,128]{2,1,0:T(8,128)S(1)}, u32[]{:S(2)}, u32[]{:S(2)}) async-start(f32[16,64,128]{2,1,0:T(8,128)} %bitcast.14), calls=%async_computation | async-start | bytes 1048576 | tf_op jit(solution)/shard_map/scatter/all_to_all | solution.py:141
  8.8 0.7 copy-start.6
  22.8 18.8 %copy-start.1 = (f32[2,4,128,128]{3,2,1,0:T(8,128)S(1)}, f32[2,4,128,128]{3,2,1,0:T(8,128)}, u32[]{:S(2)}) copy-start(f32[2,4,128,128]{3,2,1,0:T(8,128)} %orbitals.1) | copy-start | bytes 1572868
  22.9 18.8 %copy-start.2 = (f32[256,256]{1,0:T(8,128)S(1)}, f32[256,256]{1,0:T(8,128)}, u32[]{:S(2)}) copy-start(f32[256,256]{1,0:T(8,128)} %constant.24.clone.left.right) | copy-start | bytes 786436
  22.9 18.8 %copy-start.3 = (f32[256,256]{1,0:T(8,128)S(1)}, f32[256,256]{1,0:T(8,128)}, u32[]{:S(2)}) copy-start(f32[256,256]{1,0:T(8,128)} %constant.25.clone.right.left) | copy-start | bytes 786436
  22.9 18.8 %all-to-all-start.1 = ((f32[16,64,128]{2,1,0:T(8,128)}), f32[16,64,128]{2,1,0:T(8,128)S(1)}, u32[]{:S(2)}, u32[]{:S(2)}) async-start(f32[16,64,128]{2,1,0:T(8,128)} %broadcast_in_dim.8), calls=%async_computation.1 | async-start | bytes 1048576 | tf_op jit(solution)/shard_map/gather/all_to_all | solution.py:145
  46.3 44.9 %copy-start.4 = (f32[256,256]{1,0:T(8,128)S(1)}, f32[256,256]{1,0:T(8,128)}, u32[]{:S(2)}) copy-start(f32[256,256]{1,0:T(8,128)} %constant.26.clone.forward) | copy-start | bytes 786436
  46.3 44.9 %copy-start.5 = (f32[256,256]{1,0:T(8,128)S(1)}, f32[256,256]{1,0:T(8,128)}, u32[]{:S(2)}) copy-start(f32[256,256]{1,0:T(8,128)} %constant.27.clone.backward) | copy-start | bytes 786436
  46.3 44.9 %all-to-all-start.2 = ((f32[32,64,128]{2,1,0:T(8,128)}), f32[32,64,128]{2,1,0:T(8,128)S(1)}, u32[]{:S(2)}, u32[]{:S(2)}) async-start(f32[32,64,128]{2,1,0:T(8,128)} %bitcast.5), calls=%async_computation.2 | async-start | bytes 2097152 | tf_op jit(solution)/shard_map/to_columns/all_to_all | solution.py:160
where the time goes:
time: 133 us; the launch traced here: 132 us
  waiting for transfers between devices  53.1 us (40%)
  blocking collectives  33.7 us (25%)
  starting transfers between devices  31.5 us (24%)
  Pallas kernels  11.4 us (9%)
  local copies, waits for them, and re-layouts  1.71 us (1%)
    all_to_all x1, blocking collectives, body(): lax.all_to_all(spectrum.reshape(columns, rows * partners * 2 * planes, LA...  33.7 us
    all_to_all x1, waiting for transfers between devices, body(): lax.all_to_all(spectrum.reshape(columns, rows * partners * 2 * planes, LA...  28.1 us
    all_to_all x1, starting transfers between devices, body(): lax.all_to_all(spectrum.reshape(columns, rows * partners * 2 * planes, LA...  16.7 us
    all_to_all x1, waiting for transfers between devices, body(): lax.all_to_all(mine, 'band', 0, 0, tiled=True).reshape(orbitals.shape)  12.6 us
    all_to_all x1, waiting for transfers between devices, body(): pieces = lax.all_to_all(pieces, 'band', 0, 0, tiled=True)  12.4 us
    all_to_all x1, starting transfers between devices, body(): pieces = lax.all_to_all(pieces, 'band', 0, 0, tiled=True)  8.81 us
    all_to_all x1, starting transfers between devices, body(): lax.all_to_all(mine, 'band', 0, 0, tiled=True).reshape(orbitals.shape)  5.96 us
    pallas_call x1, Pallas kernels, body(): call(forward_kernel, (total, LANES), [smem()] + [vmem()] * 4, size, 'forw...  4.66 us
  transfers between devices with their start and end apart: 3, of which 3 were waited for; matrix products, arithmetic and copies ran while one was open for 0% of the time, Pallas kernels for 0%

commit v1 on v0

--- a/solution.py
+++ b/solution.py
@@ -11,6 +11,7 @@
 SCREEN = 0.025
 FRACTION = 0.25
 LANES = 128
+BATCH = 2
 VMEM_LIMIT = 40 * 1024 * 1024
 
 
@@ -39,6 +40,16 @@
 def right_product(value, matrix):
     high, low = split(value)
     return dot(high, matrix[0]) + (dot(low, matrix[0]) + dot(high, matrix[1]))
+
+
+def spread_kernel(leader, pieces, out):
+    piece = pieces[leader[0]]
+    for k in range(out.shape[0]):
+        out[k] = piece
+
+
+def tile(value, row, column, size):
+    return value[row * size : (row + 1) * size, column * size : (column + 1) * size]
 
 
 def forward_kernel(order, orbitals, received, left, right, out):
@@ -47,15 +58,22 @@
     stride = partners * 2 * planes
     left, right = split(left[...]), split(right[...])
     for j in range(partners):
-        for p in range(planes):
-            partner = received[order[j], p]
-            field = jnp.concatenate([orbitals[0, p] * partner, orbitals[1, p] * partner], axis=1)
-            along_z = right_product(field, right)
-            stacked = jnp.concatenate([along_z[:, :length], along_z[:, length:]], axis=0)
-            both = left_product(left, stacked)
-            for c in range(2):
-                row = (j * 2 + c) * planes + p
-                out[pl.ds(row, length, stride=stride), :] = both[c * length : (c + 1) * length]
+        for first in range(0, planes, BATCH):
+            group = range(first, first + BATCH)
+            fields = []
+            for p in group:
+                partner = received[order[j], p]
+                fields.append(jnp.concatenate([orbitals[c, p] * partner for c in range(2)], axis=1))
+            along_z = right_product(jnp.concatenate(fields, axis=0), right)
+            blocks = [
+                jnp.concatenate([tile(along_z, k, c, length) for k in range(BATCH)], axis=1)
+                for c in range(2)
+            ]
+            both = left_product(left, jnp.concatenate(blocks, axis=0))
+            for k, p in enumerate(group):
+                for c in range(2):
+                    row = (j * 2 + c) * planes + p
+                    out[pl.ds(row, length, stride=stride), :] = tile(both, c, k, length)
 
 
 def signed_wave(index, length):
@@ -75,36 +93,43 @@
     flat = wave_x * wave_x + wave_z * wave_z + SCREEN
     forward, backward = split(forward[...]), split(backward[...])
     factor = -FRACTION * 4.0 * math.pi / float(length**3)
+    kernels = []
     for k in range(rows):
         wave_y = signed_wave(first[0] + k, length)
-        kernel = factor / (flat + wave_y * wave_y)
-        for j in range(partners):
-            value = field[:, k, j].reshape(size, lanes)
-            value = left_product(forward, value) * kernel
-            value = left_product(backward, value)
-            out[:, k, j] = value.reshape(sources, parts, lanes)
-
-
-def backward_kernel(order, field, received, left, right, out):
+        kernels += [factor / (flat + wave_y * wave_y)] * partners
+    items = [(k, j) for k in range(rows) for j in range(partners)]
+    value = jnp.concatenate([field[:, k, j].reshape(size, lanes) for k, j in items], axis=1)
+    value = left_product(forward, value) * jnp.concatenate(kernels, axis=1)
+    value = left_product(backward, value)
+    for n, (k, j) in enumerate(items):
+        out[:, k, j] = value[:, n * lanes : (n + 1) * lanes].reshape(sources, parts, lanes)
+
+
+def backward_kernel(order, field, received, left, right, out, result, done):
     planes, length = received.shape[1], received.shape[2]
     partners = received.shape[0]
     stride = partners * 2 * planes
     left, right = split(left[...]), split(right[...])
+    copies = []
     for p in range(planes):
-        totals = None
-        for j in range(partners):
-            partner = received[order[j], p]
-            stacked = jnp.concatenate(
-                [field[pl.ds((j * 2 + c) * planes + p, length, stride=stride), :] for c in range(2)],
-                axis=0,
+        blocks = []
+        for c in range(2):
+            rows = [pl.ds((j * 2 + c) * planes + p, length, stride=stride) for j in range(partners)]
+            blocks.append(jnp.concatenate([field[row, :] for row in rows], axis=1))
+        along_y = left_product(left, jnp.concatenate(blocks, axis=0))
+        wide = [
+            jnp.concatenate([tile(along_y, c, j, length) for c in range(2)], axis=1)
+            for j in range(partners)
+        ]
+        both = right_product(jnp.concatenate(wide, axis=0), right)
+        for c in range(2):
+            result[c, p] = sum(
+                tile(both, j, c, length) * received[order[j], p] for j in range(partners)
             )
-            along_y = left_product(left, stacked)
-            wide = jnp.concatenate([along_y[:length], along_y[length:]], axis=1)
-            both = right_product(wide, right)
-            terms = [both[:, :length] * partner, both[:, length:] * partner]
-            totals = terms if totals is None else [a + b for a, b in zip(totals, terms)]
-        for c in range(2):
-            out[c, p] = totals[c]
+            copies.append(pltpu.make_async_copy(result.at[c, p], out.at[c, p], done.at[c, p]))
+            copies[-1].start()
+    for copy in copies:
+        copy.wait()
 
 
 def smem():
@@ -115,15 +140,16 @@
     return pl.BlockSpec(memory_space=pltpu.VMEM)
 
 
-def call(kernel, shape, specs, flops, name):
+def call(kernel, shape, specs, flops, name, **options):
+    options.setdefault("out_specs", vmem())
     return pl.pallas_call(
         kernel,
         out_shape=jax.ShapeDtypeStruct(shape, jnp.float32),
         in_specs=specs,
-        out_specs=vmem(),
         compiler_params=pltpu.CompilerParams(vmem_limit_bytes=VMEM_LIMIT),
         cost_estimate=pl.CostEstimate(flops=flops, bytes_accessed=4 << 20, transcendentals=0),
         name=name,
+        **options,
     )
 
 
@@ -139,8 +165,9 @@
     pieces = orbitals.reshape(groups, -1, LANES)
     with jax.named_scope("scatter"):
         pieces = lax.all_to_all(pieces, "band", 0, 0, tiled=True)
-        mine = lax.dynamic_index_in_dim(pieces, leader, 0, keepdims=True)
-        mine = jnp.broadcast_to(mine, pieces.shape)
+        mine = call(spread_kernel, pieces.shape, [smem(), vmem()], 0, "spread")(
+            leader.reshape(1), pieces
+        )
     with jax.named_scope("gather"):
         received = lax.all_to_all(mine, "band", 0, 0, tiled=True).reshape(orbitals.shape)
 
@@ -170,7 +197,16 @@
             spectrum.reshape(columns, rows * partners * 2 * planes, LANES), "fft", 0, 0, tiled=True
         )
     return call(
-        backward_kernel, orbitals.shape, [smem()] + [vmem()] * 4, size, "backward_yz"
+        backward_kernel,
+        orbitals.shape,
+        [smem()] + [vmem()] * 4,
+        size,
+        "backward_yz",
+        out_specs=pl.BlockSpec(memory_space=pl.ANY),
+        scratch_shapes=[
+            pltpu.VMEM(orbitals.shape, jnp.float32),
+            pltpu.SemaphoreType.DMA((bands, planes)),
+        ],
     )(order, spectrum.reshape(total, LANES), received, right, left)
 
 

time: 133 us -> 129 us (0.970)
  blocking collectives: 33.7 us -> 55.6 us
  waiting for transfers between devices: 53.1 us -> 40.6 us
  starting transfers between devices: 31.5 us -> 22.7 us
  Pallas kernels: 11.4 us -> 7.66 us
    all_to_all x0 -> x1, blocking collectives: none -> 21.8 us  [body(): pieces = lax.all_to_all(pieces, 'band', 0, 0, tiled=True)]
    all_to_all x1 -> x0, waiting for transfers between devices: 12.4 us -> none  [body(): pieces = lax.all_to_all(pieces, 'band', 0, 0, tiled=True)]
    all_to_all x1 -> x0, starting transfers between devices: 8.81 us -> none  [body(): pieces = lax.all_to_all(pieces, 'band', 0, 0, tiled=True)]
    pallas_call x1, Pallas kernels: 2.98 us -> 1.16 us  [body(): call(middle_kernel, shape, [smem()] + [vmem()] * 3, size, 'solve_x')]
    pallas_call x1, Pallas kernels: 4.66 us -> 2.92 us  [body(): call(forward_kernel, (total, LANES), [smem()] + [vmem()] * 4, size, 'forw...]
  transfers between devices with their start and end apart: 3 -> 2, of which waited for: 3 -> 2; matrix products, arithmetic and copies ran while one was open for 0% -> 0% of each run, Pallas kernels for 0% -> 0%
where the time goes in v1:
time: 129 us; the launch traced here: 128 us
  blocking collectives  55.6 us (43%)
  waiting for transfers between devices  40.6 us (31%)
  starting transfers between devices  22.7 us (18%)
  Pallas kernels  7.66 us (6%)
    all_to_all x1, blocking collectives, body(): lax.all_to_all(spectrum.reshape(columns, rows * partners * 2 * planes, LA...  33.7 us
    all_to_all x1, waiting for transfers between devices, body(): lax.all_to_all(spectrum.reshape(columns, rows * partners * 2 * planes, LA...  28.1 us
    all_to_all x1, blocking collectives, body(): pieces = lax.all_to_all(pieces, 'band', 0, 0, tiled=True)  21.8 us
    all_to_all x1, starting transfers between devices, body(): lax.all_to_all(spectrum.reshape(columns, rows * partners * 2 * planes, LA...  16.7 us
    all_to_all x1, waiting for transfers between devices, body(): lax.all_to_all(mine, 'band', 0, 0, tiled=True).reshape(orbitals.shape)  12.5 us
    all_to_all x1, starting transfers between devices, body(): lax.all_to_all(mine, 'band', 0, 0, tiled=True).reshape(orbitals.shape)  5.97 us
    pallas_call x1, Pallas kernels, body(): call(forward_kernel, (total, LANES), [smem()] + [vmem()] * 4, size, 'forw...  2.92 us
    pallas_call x1, Pallas kernels, body(): call(backward_kernel, orbitals.shape, [smem()] + [vmem()] * 4, size, 'bac...  2.71 us
  transfers between devices with their start and end apart: 2, of which 2 were waited for; matrix products, arithmetic and copies ran while one was open for 0% of the time, Pallas kernels for 0%

profile of v1, /device:TPU:1, one launch (start us, length us, event | category | flops | bytes accessed | tf_op | source)
XLA Modules:
  0.0 127.6 jit_solution(11359254862819023816)
XLA Ops:
  0.0 0.0 copy-start
  0.0 21.8 %all_to_all.20.pieces = f32[16,64,128]{2,1,0:T(8,128)S(1)} all-to-all(f32[16,64,128]{2,1,0:T(8,128)} %bitcast.12), channel_id=1, replica_groups=mesh['band'=16,'fft'=32] {'band'}, dimensions={0} | all-to-all | bytes 1048576 | tf_op jit(solution)/shard_map/scatter/all_to_all | solution.py:167
  21.8 0.0 copy-start.2
  21.8 0.7 copy-done.2
  22.5 0.9 spread.1
  23.4 0.0 copy-start.1
  23.4 0.0 copy-start.3
  23.4 0.0 copy-start.4
  23.4 6.0 %all-to-all-start.1 = ((f32[16,64,128]{2,1,0:T(8,128)}), f32[16,64,128]{2,1,0:T(8,128)S(1)}, u32[]{:S(2)}, u32[]{:S(2)}) async-start(f32[16,64,128]{2,1,0:T(8,128)} %spread.1), calls=%async_computation.1 | async-start | bytes 1048576 | tf_op jit(solution)/shard_map/gather/all_to_all | solution.py:172
  29.5 0.0 copy-done
  29.5 0.2 dynamic-slice_reduce_fusion.order
  29.7 12.5 %all-to-all-done.1 = f32[16,64,128]{2,1,0:T(8,128)S(1)} async-done(((f32[16,64,128]{2,1,0:T(8,128)}), f32[16,64,128]{2,1,0:T(8,128)S(1)}, u32[]{:S(2)}, u32[]{:S(2)}) %all-to-all-start.1) | async-done | bytes 524320 | tf_op jit(solution)/shard_map/gather/all_to_all | solution.py:172
  42.2 0.0 copy-done.1
  42.2 0.0 copy-done.3
  42.2 0.0 copy-done.4
  42.2 2.9 %forward_zy.1 = f32[2048,128]{1,0:T(8,128)} custom-call(s32[2]{0:T(128)S(1)} %dynamic-slice_reduce_fusion.order, f32[2,4,128,128]{3,2,1,0:T(8,128)S(1)} %copy-done.1, f32[2,4,128,128]{3,2,1,0:T(8,128)S(1)} %bitcast.13, f32[256,256]{1,0:T(8,128)S(1)} %copy-done.3, f32[256,256]{1,0:T(8,128)S(1)} %copy-done.4), custom_call_target="tpu_custom_call" | custom-call | flops 805306368 | bytes 4194304 | tf_op jit(solution)/shard_map/forward_zy/pallas_call | solution.py:183
  45.1 0.0 copy-start.5
  45.1 0.0 copy-start.6
  45.1 16.7 %all-to-all-start.2 = ((f32[32,64,128]{2,1,0:T(8,128)}), f32[32,64,128]{2,1,0:T(8,128)S(1)}, u32[]{:S(2)}, u32[]{:S(2)}) async-start(f32[32,64,128]{2,1,0:T(8,128)} %bitcast.4), calls=%async_computation.2 | async-start | bytes 2097152 | tf_op jit(solution)/shard_map/to_columns/all_to_all | solution.py:187
  61.8 28.1 %all-to-all-done.2 = f32[32,64,128]{2,1,0:T(8,128)S(1)} async-done(((f32[32,64,128]{2,1,0:T(8,128)}), f32[32,64,128]{2,1,0:T(8,128)S(1)}, u32[]{:S(2)}, u32[]{:S(2)}) %all-to-all-start.2) | async-done | bytes 1048608 | tf_op jit(solution)/shard_map/to_columns/all_to_all | solution.py:187
  90.0 0.0 copy-done.5
  90.0 0.0 copy-done.6
  90.0 1.2 solve_x.1
  91.1 33.7 %all_to_all.21 = f32[32,64,128]{2,1,0:T(8,128)S(1)} all-to-all(f32[32,64,128]{2,1,0:T(8,128)S(1)} %bitcast.11), channel_id=1, replica_groups=mesh['band'=16,'fft'=32] {'fft'}, dimensions={0} | all-to-all | bytes 2097152 | tf_op jit(solution)/shard_map/to_planes/all_to_all | solution.py:196
  124.9 2.7 %backward_yz.1 = f32[2,4,128,128]{3,2,1,0:T(8,128)} custom-call(s32[2]{0:T(128)S(1)} %dynamic-slice_reduce_fusion.order, f32[2048,128]{1,0:T(8,128)S(1)} %bitcast.10, f32[2,4,128,128]{3,2,1,0:T(8,128)S(1)} %bitcast.14, f32[256,256]{1,0:T(8,128)S(1)} %copy-done.4, f32[256,256]{1,0:T(8,128)S(1)} %copy-done.3), custom_call_target="tpu_custom_call" | custom-call | flops 805306368 | bytes 4194304 | tf_op jit(solution)/shard_map/backward_yz/pallas_call | solution.py:199
Async XLA Ops:
  0.0 29.5 %copy-start = (s32[16,2]{0,1:T(2,128)S(1)}, s32[16,2]{0,1:T(2,128)}, u32[]{:S(2)}) copy-start(s32[16,2]{0,1:T(2,128)} %param.9) | copy-start | bytes 388
  21.8 0.7 copy-start.2
  23.4 18.8 %copy-start.1 = (f32[2,4,128,128]{3,2,1,0:T(8,128)S(1)}, f32[2,4,128,128]{3,2,1,0:T(8,128)}, u32[]{:S(2)}) copy-start(f32[2,4,128,128]{3,2,1,0:T(8,128)} %orbitals.1) | copy-start | bytes 1572868
  23.4 18.8 %copy-start.3 = (f32[256,256]{1,0:T(8,128)S(1)}, f32[256,256]{1,0:T(8,128)}, u32[]{:S(2)}) copy-start(f32[256,256]{1,0:T(8,128)} %constant.20.clone.left.right) | copy-start | bytes 786436
  23.4 18.8 %copy-start.4 = (f32[256,256]{1,0:T(8,128)S(1)}, f32[256,256]{1,0:T(8,128)}, u32[]{:S(2)}) copy-start(f32[256,256]{1,0:T(8,128)} %constant.21.clone.right.left) | copy-start | bytes 786436
  23.4 18.8 %all-to-all-start.1 = ((f32[16,64,128]{2,1,0:T(8,128)}), f32[16,64,128]{2,1,0:T(8,128)S(1)}, u32[]{:S(2)}, u32[]{:S(2)}) async-start(f32[16,64,128]{2,1,0:T(8,128)} %spread.1), calls=%async_computation.1 | async-start | bytes 1048576 | tf_op jit(solution)/shard_map/gather/all_to_all | solution.py:172
  45.1 44.9 %copy-start.5 = (f32[256,256]{1,0:T(8,128)S(1)}, f32[256,256]{1,0:T(8,128)}, u32[]{:S(2)}) copy-start(f32[256,256]{1,0:T(8,128)} %constant.22.clone.forward) | copy-start | bytes 786436
  45.1 44.9 %copy-start.6 = (f32[256,256]{1,0:T(8,128)S(1)}, f32[256,256]{1,0:T(8,128)}, u32[]{:S(2)}) copy-start(f32[256,256]{1,0:T(8,128)} %constant.23.clone.backward) | copy-start | bytes 786436
  45.1 44.9 %all-to-all-start.2 = ((f32[32,64,128]{2,1,0:T(8,128)}), f32[32,64,128]{2,1,0:T(8,128)S(1)}, u32[]{:S(2)}, u32[]{:S(2)}) async-start(f32[32,64,128]{2,1,0:T(8,128)} %bitcast.4), calls=%async_computation.2 | async-start | bytes 2097152 | tf_op jit(solution)/shard_map/to_columns/all_to_all | solution.py:187

commit v2 on v1

--- a/solution.py
+++ b/solution.py
@@ -42,8 +42,8 @@
     return dot(high, matrix[0]) + (dot(low, matrix[0]) + dot(high, matrix[1]))
 
 
-def spread_kernel(leader, pieces, out):
-    piece = pieces[leader[0]]
+def spread_kernel(owner, pieces, out):
+    piece = pieces[owner[0]]
     for k in range(out.shape[0]):
         out[k] = piece
 
@@ -52,7 +52,7 @@
     return value[row * size : (row + 1) * size, column * size : (column + 1) * size]
 
 
-def forward_kernel(order, orbitals, received, left, right, out):
+def forward_kernel(owner, occupied, orbitals, received, left, right, out):
     planes, length = orbitals.shape[1], orbitals.shape[2]
     partners = received.shape[0]
     stride = partners * 2 * planes
@@ -62,7 +62,7 @@
             group = range(first, first + BATCH)
             fields = []
             for p in group:
-                partner = received[order[j], p]
+                partner = received[occupied[j, owner[0]], p]
                 fields.append(jnp.concatenate([orbitals[c, p] * partner for c in range(2)], axis=1))
             along_z = right_product(jnp.concatenate(fields, axis=0), right)
             blocks = [
@@ -81,7 +81,7 @@
     return signed.astype(jnp.float32) * (2.0 * math.pi / length)
 
 
-def middle_kernel(first, field, forward, backward, out):
+def middle_kernel(field, forward, backward, out):
     sources, rows, partners, parts, lanes = field.shape
     planes = parts // 2
     length = sources * planes
@@ -95,7 +95,7 @@
     factor = -FRACTION * 4.0 * math.pi / float(length**3)
     kernels = []
     for k in range(rows):
-        wave_y = signed_wave(first[0] + k, length)
+        wave_y = signed_wave(lax.axis_index("fft") * rows + k, length)
         kernels += [factor / (flat + wave_y * wave_y)] * partners
     items = [(k, j) for k in range(rows) for j in range(partners)]
     value = jnp.concatenate([field[:, k, j].reshape(size, lanes) for k, j in items], axis=1)
@@ -105,7 +105,7 @@
         out[:, k, j] = value[:, n * lanes : (n + 1) * lanes].reshape(sources, parts, lanes)
 
 
-def backward_kernel(order, field, received, left, right, out, result, done):
+def backward_kernel(owner, occupied, field, received, left, right, out, result, done):
     planes, length = received.shape[1], received.shape[2]
     partners = received.shape[0]
     stride = partners * 2 * planes
@@ -124,7 +124,7 @@
         both = right_product(jnp.concatenate(wide, axis=0), right)
         for c in range(2):
             result[c, p] = sum(
-                tile(both, j, c, length) * received[order[j], p] for j in range(partners)
+                tile(both, j, c, length) * received[occupied[j, owner[0]], p] for j in range(partners)
             )
             copies.append(pltpu.make_async_copy(result.at[c, p], out.at[c, p], done.at[c, p]))
             copies[-1].start()
@@ -159,14 +159,12 @@
     columns = lax.axis_size("fft")
     rows = length // columns
     partners = occupied.shape[1]
-    leader = owner[0]
-    order = lax.dynamic_index_in_dim(occupied, leader, 0, keepdims=False)
 
     pieces = orbitals.reshape(groups, -1, LANES)
     with jax.named_scope("scatter"):
         pieces = lax.all_to_all(pieces, "band", 0, 0, tiled=True)
         mine = call(spread_kernel, pieces.shape, [smem(), vmem()], 0, "spread")(
-            leader.reshape(1), pieces
+            owner, pieces
         )
     with jax.named_scope("gather"):
         received = lax.all_to_all(mine, "band", 0, 0, tiled=True).reshape(orbitals.shape)
@@ -181,17 +179,16 @@
     size = 3 * 2 * 2 * length * 2 * length * partners * planes * length * 2
     total = length * partners * 2 * planes
     spectrum = call(
-        forward_kernel, (total, LANES), [smem()] + [vmem()] * 4, size, "forward_zy"
-    )(order, orbitals, received, left, right)
+        forward_kernel, (total, LANES), [smem()] * 2 + [vmem()] * 4, size, "forward_zy"
+    )(owner, occupied.T, orbitals, received, left, right)
     with jax.named_scope("to_columns"):
         spectrum = lax.all_to_all(
             spectrum.reshape(columns, rows * partners * 2 * planes, LANES), "fft", 0, 0, tiled=True
         )
-    first = (lax.axis_index("fft") * rows).astype(jnp.int32).reshape(1)
     shape = (columns, rows, partners, 2 * planes, LANES)
     spectrum = call(
-        middle_kernel, shape, [smem()] + [vmem()] * 3, size, "solve_x"
-    )(first, spectrum.reshape(shape), x_forward, x_backward)
+        middle_kernel, shape, [vmem()] * 3, size, "solve_x"
+    )(spectrum.reshape(shape), x_forward, x_backward)
     with jax.named_scope("to_planes"):
         spectrum = lax.all_to_all(
             spectrum.reshape(columns, rows * partners * 2 * planes, LANES), "fft", 0, 0, tiled=True
@@ -199,7 +196,7 @@
     return call(
         backward_kernel,
         orbitals.shape,
-        [smem()] + [vmem()] * 4,
+        [smem()] * 2 + [vmem()] * 4,
         size,
         "backward_yz",
         out_specs=pl.BlockSpec(memory_space=pl.ANY),
@@ -207,7 +204,7 @@
             pltpu.VMEM(orbitals.shape, jnp.float32),
             pltpu.SemaphoreType.DMA((bands, planes)),
         ],
-    )(order, spectrum.reshape(total, LANES), received, right, left)
+    )(owner, occupied.T, spectrum.reshape(total, LANES), received, right, left)
 
 
 def solution(mesh):

time: 129 us -> 127 us (0.984)
  blocking collectives: 55.6 us -> 119 us
  waiting for transfers between devices: 40.6 us -> 0 us
  starting transfers between devices: 22.7 us -> 0 us
  Pallas kernels: 7.66 us -> 6.35 us
    all_to_all x1 -> x2, blocking collectives: 33.7 us -> 78.4 us  [body(): lax.all_to_all(spectrum.reshape(columns, rows * partners * 2 * planes, LA...]
    all_to_all x2 -> x0, waiting for transfers between devices: 40.6 us -> none  [the longest x1 28.1 us: body(): lax.all_to_all(spectrum.reshape(columns, rows * partners * 2 * planes, LA...]
    all_to_all x2 -> x0, starting transfers between devices: 22.7 us -> none  [the longest x1 16.7 us: body(): lax.all_to_all(spectrum.reshape(columns, rows * partners * 2 * planes, LA...]
    all_to_all x0 -> x1, blocking collectives: none -> 18.6 us  [body(): lax.all_to_all(mine, 'band', 0, 0, tiled=True).reshape(orbitals.shape)]
  transfers between devices with their start and end apart: 2 -> 0, of which waited for: 2 -> 0; matrix products, arithmetic and copies ran while one was open for 0% -> 0% of each run, Pallas kernels for 0% -> 0%
where the time goes in v2:
time: 127 us; the launch traced here: 126 us
  blocking collectives  119 us (94%)
  Pallas kernels  6.35 us (5%)
    all_to_all x2, blocking collectives, body(): lax.all_to_all(spectrum.reshape(columns, rows * partners * 2 * planes, LA...  78.4 us
    all_to_all x1, blocking collectives, body(): pieces = lax.all_to_all(pieces, 'band', 0, 0, tiled=True)  22 us
    all_to_all x1, blocking collectives, body(): lax.all_to_all(mine, 'band', 0, 0, tiled=True).reshape(orbitals.shape)  18.6 us
    pallas_call x1, Pallas kernels, body(): call(backward_kernel, orbitals.shape, [smem()] * 2 + [vmem()] * 4, size,...  2.69 us

profile of v2, /device:TPU:1, one launch (start us, length us, event | category | flops | bytes accessed | tf_op | source)
XLA Modules:
  0.0 126.1 jit_solution(953007666870594278)
XLA Ops:
  0.0 0.0 copy-start.1
  0.0 22.0 %all_to_all.20.pieces = f32[16,64,128]{2,1,0:T(8,128)S(1)} all-to-all(f32[16,64,128]{2,1,0:T(8,128)} %bitcast.11), channel_id=1, replica_groups=mesh['band'=16,'fft'=32] {'band'}, dimensions={0} | all-to-all | bytes 1048576 | tf_op jit(solution)/shard_map/scatter/all_to_all | solution.py:165
  22.0 0.0 copy-done.1
  22.0 0.6 spread.1
  22.6 0.0 copy-start
  22.6 0.0 copy-start.3
  22.6 0.0 copy-start.4
  22.6 18.6 %all_to_all.21 = f32[16,64,128]{2,1,0:T(8,128)S(1)} all-to-all(f32[16,64,128]{2,1,0:T(8,128)S(1)} %spread.1), channel_id=1, replica_groups=mesh['band'=16,'fft'=32] {'band'}, dimensions={0} | all-to-all | bytes 1048576 | tf_op jit(solution)/shard_map/gather/all_to_all | solution.py:170
  41.2 0.0 copy-start.2
  41.2 0.0 copy-done
  41.2 0.0 copy-done.3
  41.2 0.0 copy-done.4
  41.2 0.7 copy-done.2
  41.9 2.0 %forward_zy.1 = f32[2048,128]{1,0:T(8,128)S(1)} custom-call(s32[4]{0:T(128)S(1)} %copy-done.1, s32[2,16]{1,0:T(2,128)S(1)} %bitcast.14, f32[2,4,128,128]{3,2,1,0:T(8,128)S(1)} %copy-done, f32[2,4,128,128]{3,2,1,0:T(8,128)S(1)} %bitcast.12, f32[256,256]{1,0:T(8,128)S(1)} %copy-done.4, f32[256,256]{1,0:T(8,128)S(1)} %copy-done.3), custom_call_target="tpu_custom_call" | custom-call | flops 805306368 | bytes 4194304 | tf_op jit(solution)/shard_map/forward_zy/pallas_call | solution.py:181
  43.8 0.0 copy-start.5
  43.8 0.0 copy-start.6
  43.8 44.7 %all_to_all.22 = f32[32,64,128]{2,1,0:T(8,128)S(1)} all-to-all(f32[32,64,128]{2,1,0:T(8,128)S(1)} %bitcast.10), channel_id=1, replica_groups=mesh['band'=16,'fft'=32] {'fft'}, dimensions={0} | all-to-all | bytes 2097152 | tf_op jit(solution)/shard_map/to_columns/all_to_all | solution.py:185
  88.5 0.0 copy-done.5
  88.5 0.0 copy-done.6
  88.5 1.1 solve_x.1
  89.6 33.7 %all_to_all.23 = f32[32,64,128]{2,1,0:T(8,128)S(1)} all-to-all(f32[32,64,128]{2,1,0:T(8,128)S(1)} %bitcast.9), channel_id=1, replica_groups=mesh['band'=16,'fft'=32] {'fft'}, dimensions={0} | all-to-all | bytes 2097152 | tf_op jit(solution)/shard_map/to_planes/all_to_all | solution.py:193
  123.4 2.7 %backward_yz.1 = f32[2,4,128,128]{3,2,1,0:T(8,128)} custom-call(s32[4]{0:T(128)S(1)} %copy-done.1, s32[2,16]{1,0:T(2,128)S(1)} %bitcast.15, f32[2048,128]{1,0:T(8,128)S(1)} %bitcast.7, f32[2,4,128,128]{3,2,1,0:T(8,128)S(1)} %bitcast.13, f32[256,256]{1,0:T(8,128)S(1)} %copy-done.3, f32[256,256]{1,0:T(8,128)S(1)} %copy-done.4), custom_call_target="tpu_custom_call" | custom-call | flops 805306368 | bytes 4194304 | tf_op jit(solution)/shard_map/backward_yz/pallas_call | solution.py:196
Async XLA Ops:
  0.0 22.0 %copy-start.1 = (s32[4]{0:T(128)S(1)}, s32[4]{0:T(128)}, u32[]{:S(2)}) copy-start(s32[4]{0:T(128)} %owner.5) | copy-start | bytes 52
  22.6 18.6 %copy-start = (f32[2,4,128,128]{3,2,1,0:T(8,128)S(1)}, f32[2,4,128,128]{3,2,1,0:T(8,128)}, u32[]{:S(2)}) copy-start(f32[2,4,128,128]{3,2,1,0:T(8,128)} %orbitals.1) | copy-start | bytes 1572868
  22.6 18.6 %copy-start.3 = (f32[256,256]{1,0:T(8,128)S(1)}, f32[256,256]{1,0:T(8,128)}, u32[]{:S(2)}) copy-start(f32[256,256]{1,0:T(8,128)} %constant.9.clone.right.left) | copy-start | bytes 786436
  22.6 18.6 %copy-start.4 = (f32[256,256]{1,0:T(8,128)S(1)}, f32[256,256]{1,0:T(8,128)}, u32[]{:S(2)}) copy-start(f32[256,256]{1,0:T(8,128)} %constant.8.clone.left.right) | copy-start | bytes 786436
  41.2 0.7 copy-start.2
  43.8 44.7 %copy-start.5 = (f32[256,256]{1,0:T(8,128)S(1)}, f32[256,256]{1,0:T(8,128)}, u32[]{:S(2)}) copy-start(f32[256,256]{1,0:T(8,128)} %constant.11.clone.backward) | copy-start | bytes 786436
  43.8 44.7 %copy-start.6 = (f32[256,256]{1,0:T(8,128)S(1)}, f32[256,256]{1,0:T(8,128)}, u32[]{:S(2)}) copy-start(f32[256,256]{1,0:T(8,128)} %constant.10.clone.forward) | copy-start | bytes 786436

commit v3 on v2

v3 whole, which is shorter than its diff:
```python
import math

import jax
import jax.numpy as jnp
import numpy as np
from jax import lax
from jax.experimental import pallas as pl
from jax.experimental.pallas import tpu as pltpu
from jax.sharding import PartitionSpec as P

SCREEN = 0.025
FRACTION = 0.25
LANES = 128
BATCH = 2
RING = 8
VMEM_LIMIT = 40 * 1024 * 1024


def wave_matrix(length):
    indices = np.arange(length)
    angles = (indices[:, None] * indices[None, :] % length) * (2.0 * math.pi / length)
    cosine, sine = np.cos(angles), np.sin(angles)
    return np.block([[cosine, sine], [-sine, cosine]]).astype(np.float32)


def split(value):
    high = value.astype(jnp.bfloat16)
    low = (value - high.astype(jnp.float32)).astype(jnp.bfloat16)
    return high, low


def dot(left, right):
    return jnp.dot(left, right, preferred_element_type=jnp.float32)


def left_product(matrix, value):
    high, low = split(value)
    return dot(matrix[0], high) + (dot(matrix[0], low) + dot(matrix[1], high))


def right_product(value, matrix):
    high, low = split(value)
    return dot(high, matrix[0]) + (dot(low, matrix[0]) + dot(high, matrix[1]))


def spread_kernel(owner, occupied, pieces, out):
    piece = pieces[owner[0]]
    for k in range(out.shape[0]):
        out[k] = piece


def tile(value, row, column, size):
    return value[row * size : (row + 1) * size, column * size : (column + 1) * size]


def forward_kernel(own, other, received, left, right, out):
    planes, length = received.shape[0], received.shape[1]
    stride = 2 * 2 * planes
    left, right = split(left[...]), split(right[...])
    for s, orbitals in enumerate((own, other)):
        for first in range(0, planes, BATCH):
            group = range(first, first + BATCH)
            fields = []
            for p in group:
                partner = received[p]
                fields.append(jnp.concatenate([orbitals[c, p] * partner for c in range(2)], axis=1))
            along_z = right_product(jnp.concatenate(fields, axis=0), right)
            blocks = [
                jnp.concatenate([tile(along_z, k, c, length) for k in range(BATCH)], axis=1)
                for c in range(2)
            ]
            both = left_product(left, jnp.concatenate(blocks, axis=0))
            for k, p in enumerate(group):
                for c in range(2):
                    row = (s * 2 + c) * planes + p
                    out[pl.ds(row, length, stride=stride), :] = tile(both, c, k, length)


def signed_wave(index, length):
    signed = jnp.where(index <= length // 2, index, index - length)
    return signed.astype(jnp.float32) * (2.0 * math.pi / length)


def middle_kernel(owner, occupied, field, forward, backward, out):
    sources, rows, fields, parts, lanes = field.shape
    planes = parts // 2
    length = sources * planes
    size = sources * parts
    ring = lax.axis_index("band") // RING
    weight = sum((occupied[j, owner[0]] == ring).astype(jnp.float32) for j in range(occupied.shape[0]))
    factor = weight * (-FRACTION * 4.0 * math.pi / float(length**3))
    row = lax.broadcasted_iota(jnp.int32, (size, lanes), 0)
    x_index = (row // parts) * planes + row % planes
    wave_x = signed_wave(x_index, length)
    wave_z = signed_wave(lax.broadcasted_iota(jnp.int32, (size, lanes), 1), length)
    flat = wave_x * wave_x + wave_z * wave_z + SCREEN
    forward, backward = split(forward[...]), split(backward[...])
    kernels = []
    for k in range(rows):
        wave_y = signed_wave(lax.axis_index("fft") * rows + k, length)
        kernels += [factor / (flat + wave_y * wave_y)] * fields
    items = [(k, s) for k in range(rows) for s in range(fields)]
    value = jnp.concatenate([field[:, k, s].reshape(size, lanes) for k, s in items], axis=1)
    value = left_product(forward, value) * jnp.concatenate(kernels, axis=1)
    value = left_product(backward, value)
    for n, (k, s) in enumerate(items):
        target = ring if s == 0 else 1 - ring
        part = value[:, n * lanes : (n + 1) * lanes]
        out[target, :, k] = part.reshape(sources, parts, lanes)


def backward_kernel(field, own, other, left, right, out, result, done):
    planes, length = own.shape[0], own.shape[1]
    ring = lax.axis_index("band") // RING
    partners = ((ring, own), (1 - ring, other))
    left, right = split(left[...]), split(right[...])
    copies = []
    for p in range(planes):
        blocks = []
        for c in range(2):
            rows = pl.ds(c * planes + p, length, stride=2 * planes)
            blocks.append(jnp.concatenate([field[j, rows, :] for j, _ in partners], axis=1))
        along_y = left_product(left, jnp.concatenate(blocks, axis=0))
        wide = [
            jnp.concatenate([tile(along_y, c, k, length) for c in range(2)], axis=1)
            for k in range(len(partners))
        ]
        both = right_product(jnp.concatenate(wide, axis=0), right)
        for c in range(2):
            result[c, p] = sum(
                tile(both, k, c, length) * partner[p] for k, (_, partner) in enumerate(partners)
            )
            copies.append(pltpu.make_async_copy(result.at[c, p], out.at[c, p], done.at[c, p]))
            copies[-1].start()
    for copy in copies:
        copy.wait()


def smem():
    return pl.BlockSpec(memory_space=pltpu.SMEM)


def vmem():
    return pl.BlockSpec(memory_space=pltpu.VMEM)


def call(kernel, shape, specs, flops, name, **options):
    options.setdefault("out_specs", vmem())
    return pl.pallas_call(
        kernel,
        out_shape=jax.ShapeDtypeStruct(shape, jnp.float32),
        in_specs=specs,
        compiler_params=pltpu.CompilerParams(vmem_limit_bytes=VMEM_LIMIT),
        cost_estimate=pl.CostEstimate(flops=flops, bytes_accessed=4 << 20, transcendentals=0),
        name=name,
        **options,
    )


def body(orbitals, owner, occupied):
    bands, planes, length, _ = orbitals.shape
    groups = lax.axis_size("band")
    columns = lax.axis_size("fft")
    rows = length // columns
    ring = RING
    order = occupied.T
    flops = 2 * 2 * 3 * 2 * (2 * length) * (2 * length) * planes * length

    swap = [(k, (k + ring) % groups) for k in range(groups)]
    with jax.named_scope("swap_orbitals"):
        other = lax.ppermute(orbitals, "band", swap)

    with jax.named_scope("scatter"):
        pieces = lax.all_to_all(orbitals.reshape(groups, -1, LANES), "band", 0, 0, tiled=True)
    mine = call(
        spread_kernel, (ring,) + pieces.shape[1:], [smem()] * 2 + [vmem()], 0, "spread"
    )(owner, order, pieces)
    rings = [[a * ring + y for y in range(ring)] for a in range(2)]
    with jax.named_scope("gather"):
        received = lax.all_to_all(mine, "band", 0, 0, axis_index_groups=rings, tiled=True)
    received = received.reshape(planes, length, length)

    matrix = wave_matrix(length)
    left, right = matrix, matrix.T.copy()
    x_index = np.arange(length).reshape(columns, 1, planes) + np.array([0, length])[None, :, None]
    x_index = x_index.reshape(-1)
    mixed = matrix[np.ix_(x_index, x_index)]
    x_forward, x_backward = mixed, mixed.T.copy()

    spectrum = call(
        forward_kernel, (length * 2 * 2 * planes, LANES), [vmem()] * 5, flops, "forward_zy"
    )(orbitals, other, received, left, right)
    with jax.named_scope("to_columns"):
        spectrum = lax.all_to_all(
            spectrum.reshape(columns, rows * 2 * 2 * planes, LANES), "fft", 0, 0, tiled=True
        )
    with jax.named_scope("swap_received"):
        received_other = lax.ppermute(received, "band", swap)
    spectrum = call(
        middle_kernel,
        (2, columns, rows, 2 * planes, LANES),
        [smem()] * 2 + [vmem()] * 3,
        flops,
        "solve_x",
    )(owner, order, spectrum.reshape(columns, rows, 2, 2 * planes, LANES), x_forward, x_backward)
    sharing = [
        [(a * ring + y) * columns + f for a in range(2) for f in range(columns)] for y in range(ring)
    ]
    with jax.named_scope("to_planes"):
        spectrum = lax.all_to_all(
            spectrum.reshape(2 * columns, rows * 2 * planes, LANES),
            ("band", "fft"),
            0,
            0,
            axis_index_groups=sharing,
            tiled=True,
        )
    return call(
        backward_kernel,
        orbitals.shape,
        [vmem()] * 5,
        flops,
        "backward_yz",
        out_specs=pl.BlockSpec(memory_space=pl.ANY),
        scratch_shapes=[
            pltpu.VMEM(orbitals.shape, jnp.float32),
            pltpu.SemaphoreType.DMA((bands, planes)),
        ],
    )(
        spectrum.reshape(2, columns * rows * 2 * planes, LANES),
        received,
        received_other,
        right,
        left,
    )


def solution(mesh):
    return jax.shard_map(
        body,
        mesh=mesh,
        in_specs=(P("band", "fft", None, None), P(), P()),
        out_specs=P("band", "fft", None, None),
        check_vma=False,
    )
```

time: 127 us -> 124 us (0.976)
  blocking collectives: 119 us -> 44.7 us
  waiting for transfers between devices: 0 us -> 43.8 us
  starting transfers between devices: 0 us -> 27 us
    all_to_all x4 -> x1, blocking collectives: 119 us -> 44.7 us  [body(): lax.all_to_all(spectrum.reshape(columns, rows * 2 * 2 * planes, LANES), '...]
    all_to_all x0 -> x3, waiting for transfers between devices: none -> 33.2 us  [the longest x1 14.1 us: body(): lax.all_to_all(spectrum.reshape(2 * columns, rows * 2 * planes, LANES), (...]
    all_to_all x0 -> x3, starting transfers between devices: none -> 20.3 us  [the longest x1 8.81 us: body(): lax.all_to_all(orbitals.reshape(groups, -1, LANES), 'band', 0, 0, tiled=T...]
    ppermute x0 -> x2, waiting for transfers between devices: none -> 10.6 us  [the longest x1 10.5 us: body(): received_other = lax.ppermute(received, 'band', swap)]
    ppermute x0 -> x2, starting transfers between devices: none -> 6.67 us  [the longest x1 3.39 us: body(): received_other = lax.ppermute(received, 'band', swap)]
  transfers between devices with their start and end apart: 0 -> 5, of which waited for: 0 -> 5; matrix products, arithmetic and copies ran while one was open for 0% -> 0% of each run, Pallas kernels for 0% -> 1%
where the time goes in v3:
time: 124 us; the launch traced here: 123 us
  blocking collectives  44.7 us (36%)
  waiting for transfers between devices  43.8 us (35%)
  starting transfers between devices  27 us (22%)
  Pallas kernels  7.48 us (6%)
    all_to_all x1, blocking collectives, body(): lax.all_to_all(spectrum.reshape(columns, rows * 2 * 2 * planes, LANES), '...  44.7 us
    all_to_all x1, waiting for transfers between devices, body(): lax.all_to_all(spectrum.reshape(2 * columns, rows * 2 * planes, LANES), (...  14.1 us
    ppermute x1, waiting for transfers between devices, body(): received_other = lax.ppermute(received, 'band', swap)  10.5 us
    all_to_all x1, waiting for transfers between devices, body(): lax.all_to_all(orbitals.reshape(groups, -1, LANES), 'band', 0, 0, tiled=T...  9.86 us
    all_to_all x1, waiting for transfers between devices, body(): lax.all_to_all(mine, 'band', 0, 0, axis_index_groups=rings, tiled=True)  9.21 us
    all_to_all x1, starting transfers between devices, body(): lax.all_to_all(orbitals.reshape(groups, -1, LANES), 'band', 0, 0, tiled=T...  8.81 us
    all_to_all x1, starting transfers between devices, body(): lax.all_to_all(spectrum.reshape(2 * columns, rows * 2 * planes, LANES), (...  6.2 us
    all_to_all x1, starting transfers between devices, body(): lax.all_to_all(mine, 'band', 0, 0, axis_index_groups=rings, tiled=True)  5.31 us
  transfers between devices with their start and end apart: 5, of which 5 were waited for; matrix products, arithmetic and copies ran while one was open for 0% of the time, Pallas kernels for 1%

profile of v3, /device:TPU:1, one launch (start us, length us, event | category | flops | bytes accessed | tf_op | source)
XLA Modules:
  0.0 123.1 jit_solution(10588470227530588253)
XLA Ops:
  0.0 0.0 copy-start
  0.0 8.8 %all-to-all-start = ((f32[16,64,128]{2,1,0:T(8,128)}), f32[16,64,128]{2,1,0:T(8,128)S(1)}, u32[]{:S(2)}, u32[]{:S(2)}) async-start(f32[16,64,128]{2,1,0:T(8,128)} %bitcast.10), calls=%async_computation | async-start | bytes 1048576 | tf_op jit(solution)/shard_map/scatter/all_to_all | solution.py:174
  8.8 0.0 copy-done
  8.8 0.0 copy-start.1
  8.8 0.0 copy-start.2
  8.9 3.3 %collective-permute-start = (f32[2,4,128,128]{3,2,1,0:T(8,128)S(1)}, f32[2,4,128,128]{3,2,1,0:T(8,128)S(1)}, u32[]{:S(2)}, u32[]{:S(2)}) collective-permute-start(f32[2,4,128,128]{3,2,1,0:T(8,128)S(1)} %copy-done), channel_id=1, source_target_pairs={{0,256},{32,288},{64,320},{96,352},{128,384},{160,416},{192,448},{... | collective-permute-start | bytes 1572872 | tf_op jit(solution)/shard_map/swap_orbitals/ppermute | solution.py:171
  12.1 9.9 %all-to-all-done.pieces = f32[16,64,128]{2,1,0:T(8,128)S(1)} async-done(((f32[16,64,128]{2,1,0:T(8,128)}), f32[16,64,128]{2,1,0:T(8,128)S(1)}, u32[]{:S(2)}, u32[]{:S(2)}) %all-to-all-start) | async-done | bytes 524320 | tf_op jit(solution)/shard_map/scatter/all_to_all | solution.py:174
  22.0 0.0 copy-done.1
  22.0 0.0 copy-done.2
  22.0 1.3 %spread.1 = f32[8,64,128]{2,1,0:T(8,128)} custom-call(s32[4]{0:T(128)S(1)} %copy-done.2, s32[2,16]{1,0:T(2,128)S(1)} %bitcast.14, f32[16,64,128]{2,1,0:T(8,128)S(1)} %all-to-all-done.pieces), custom_call_target="tpu_custom_call" | custom-call | bytes 4194304 | tf_op jit(solution)/shard_map/spread/pallas_call | solution.py:175
  23.3 0.0 copy-start.3
  23.3 0.0 copy-start.4
  23.3 5.3 %all-to-all-start.1 = ((f32[8,64,128]{2,1,0:T(8,128)}), f32[8,64,128]{2,1,0:T(8,128)S(1)}, u32[]{:S(2)}, u32[]{:S(2)}) async-start(f32[8,64,128]{2,1,0:T(8,128)} %spread.1), calls=%async_computation.1 | async-start | bytes 524288 | tf_op jit(solution)/shard_map/gather/all_to_all | solution.py:180
  28.6 0.1 collective-permute-done.other
  28.7 9.2 %all-to-all-done.1 = f32[8,64,128]{2,1,0:T(8,128)S(1)} async-done(((f32[8,64,128]{2,1,0:T(8,128)}), f32[8,64,128]{2,1,0:T(8,128)S(1)}, u32[]{:S(2)}, u32[]{:S(2)}) %all-to-all-start.1) | async-done | bytes 262176 | tf_op jit(solution)/shard_map/gather/all_to_all | solution.py:180
  37.9 0.0 copy-done.3
  37.9 0.0 copy-done.4
  37.9 1.4 %forward_zy.1 = f32[2048,128]{1,0:T(8,128)S(1)} custom-call(f32[2,4,128,128]{3,2,1,0:T(8,128)S(1)} %copy-done, f32[2,4,128,128]{3,2,1,0:T(8,128)S(1)} %collective-permute-done.other, f32[4,128,128]{2,1,0:T(8,128)S(1)} %bitcast.11, f32[256,256]{1,0:T(8,128)S(1)} %copy-done.3, f32[256,256]{1,0:T(8,128)S(1)} %copy-done.4), custom_call_target="tpu_custom_call" | custom-call | flops 805306368 | bytes 4194304 | tf_op jit(solution)/shard_map/forward_zy/pallas_call | solution.py:190
  39.3 0.0 copy-start.5
  39.4 0.0 copy-start.6
  39.4 44.7 %all_to_all.20 = f32[32,64,128]{2,1,0:T(8,128)S(1)} all-to-all(f32[32,64,128]{2,1,0:T(8,128)S(1)} %bitcast.9), channel_id=1, replica_groups=mesh['band'=16,'fft'=32] {'fft'}, dimensions={0} | all-to-all | bytes 2097152 | tf_op jit(solution)/shard_map/to_columns/all_to_all | solution.py:194
  84.1 0.0 copy-done.5
  84.1 0.0 copy-done.6
  84.1 2.7 %solve_x.1 = f32[2,32,4,8,128]{4,3,2,1,0:T(8,128)} custom-call(s32[4]{0:T(128)S(1)} %copy-done.2, s32[2,16]{1,0:T(2,128)S(1)} %bitcast.15, f32[32,4,2,8,128]{4,3,2,1,0:T(8,128)S(1)} %bitcast.8, f32[256,256]{1,0:T(8,128)S(1)} %copy-done.5, f32[256,256]{1,0:T(8,128)S(1)} %copy-done.6), custom_call_target="tpu_custom_call" | custom-call | flops 805306368 | bytes 4194304 | tf_op jit(solution)/shard_map/solve_x/pallas_call | solution.py:199
  86.8 6.2 %all-to-all-start.3 = ((f32[64,32,128]{2,1,0:T(8,128)}), f32[64,32,128]{2,1,0:T(8,128)S(1)}, u32[]{:S(2)}, u32[]{:S(2)}) async-start(f32[64,32,128]{2,1,0:T(8,128)} %bitcast.5), calls=%async_computation.3 | async-start | bytes 2097152 | tf_op jit(solution)/shard_map/to_planes/all_to_all | solution.py:210
  93.0 3.4 %collective-permute-start.1 = (f32[4,128,128]{2,1,0:T(8,128)S(1)}, f32[4,128,128]{2,1,0:T(8,128)S(1)}, u32[]{:S(2)}, u32[]{:S(2)}) collective-permute-start(f32[4,128,128]{2,1,0:T(8,128)S(1)} %bitcast.12), channel_id=1, source_target_pairs={{0,256},{32,288},{64,320},{96,352},{128,384},{160,416},{192,448},{... | collective-permute-start | bytes 786440 | tf_op jit(solution)/shard_map/swap_received/ppermute | solution.py:198
  96.4 10.5 %collective-permute-done.1.other = f32[4,128,128]{2,1,0:T(8,128)S(1)} collective-permute-done((f32[4,128,128]{2,1,0:T(8,128)S(1)}, f32[4,128,128]{2,1,0:T(8,128)S(1)}, u32[]{:S(2)}, u32[]{:S(2)}) %collective-permute-start.1) | collective-permute-done | bytes 262176 | tf_op jit(solution)/shard_map/swap_received/ppermute | solution.py:198
  106.9 14.1 %all-to-all-done.3 = f32[64,32,128]{2,1,0:T(8,128)S(1)} async-done(((f32[64,32,128]{2,1,0:T(8,128)}), f32[64,32,128]{2,1,0:T(8,128)S(1)}, u32[]{:S(2)}, u32[]{:S(2)}) %all-to-all-start.3) | async-done | bytes 1048608 | tf_op jit(solution)/shard_map/to_planes/all_to_all | solution.py:210
  121.1 2.1 %backward_yz.1 = f32[2,4,128,128]{3,2,1,0:T(8,128)} custom-call(f32[2,1024,128]{2,1,0:T(8,128)S(1)} %bitcast.7, f32[4,128,128]{2,1,0:T(8,128)S(1)} %bitcast.13, f32[4,128,128]{2,1,0:T(8,128)S(1)} %collective-permute-done.1.other, f32[256,256]{1,0:T(8,128)S(1)} %copy-done.4, f32[256,256]{1,0:T(8,128)S(1)} %copy-done.3), custom_call_target="tpu_custom_call" | custom-call | flops 805306368 | bytes 4194304 | tf_op jit(solution)/shard_map/backward_yz/pallas_call | solution.py:218
Async XLA Ops:
  0.0 8.8 %copy-start = (f32[2,4,128,128]{3,2,1,0:T(8,128)S(1)}, f32[2,4,128,128]{3,2,1,0:T(8,128)}, u32[]{:S(2)}) copy-start(f32[2,4,128,128]{3,2,1,0:T(8,128)} %own.1) | copy-start | bytes 1572868
  0.0 22.0 %all-to-all-start = ((f32[16,64,128]{2,1,0:T(8,128)}), f32[16,64,128]{2,1,0:T(8,128)S(1)}, u32[]{:S(2)}, u32[]{:S(2)}) async-start(f32[16,64,128]{2,1,0:T(8,128)} %bitcast.10), calls=%async_computation | async-start | bytes 1048576 | tf_op jit(solution)/shard_map/scatter/all_to_all | solution.py:174
  8.8 13.2 %copy-start.1 = (s32[16,2]{0,1:T(2,128)S(1)}, s32[16,2]{0,1:T(2,128)}, u32[]{:S(2)}) copy-start(s32[16,2]{0,1:T(2,128)} %param.9) | copy-start | bytes 388
  8.8 13.2 %copy-start.2 = (s32[4]{0:T(128)S(1)}, s32[4]{0:T(128)}, u32[]{:S(2)}) copy-start(s32[4]{0:T(128)} %owner.3) | copy-start | bytes 52
  8.9 19.8 %collective-permute-start = (f32[2,4,128,128]{3,2,1,0:T(8,128)S(1)}, f32[2,4,128,128]{3,2,1,0:T(8,128)S(1)}, u32[]{:S(2)}, u32[]{:S(2)}) collective-permute-start(f32[2,4,128,128]{3,2,1,0:T(8,128)S(1)} %copy-done), channel_id=1, source_target_pairs={{0,256},{32,288},{64,320},{96,352},{128,384},{160,416},{192,448},{... | collective-permute-start | bytes 1572872 | tf_op jit(solution)/shard_map/swap_orbitals/ppermute | solution.py:171
  23.3 14.6 %copy-start.3 = (f32[256,256]{1,0:T(8,128)S(1)}, f32[256,256]{1,0:T(8,128)}, u32[]{:S(2)}) copy-start(f32[256,256]{1,0:T(8,128)} %constant.8.clone.left.right) | copy-start | bytes 786436
  23.3 14.6 %copy-start.4 = (f32[256,256]{1,0:T(8,128)S(1)}, f32[256,256]{1,0:T(8,128)}, u32[]{:S(2)}) copy-start(f32[256,256]{1,0:T(8,128)} %constant.9.clone.right.left) | copy-start | bytes 786436
  23.3 14.6 %all-to-all-start.1 = ((f32[8,64,128]{2,1,0:T(8,128)}), f32[8,64,128]{2,1,0:T(8,128)S(1)}, u32[]{:S(2)}, u32[]{:S(2)}) async-start(f32[8,64,128]{2,1,0:T(8,128)} %spread.1), calls=%async_computation.1 | async-start | bytes 524288 | tf_op jit(solution)/shard_map/gather/all_to_all | solution.py:180
  39.3 44.7 %copy-start.5 = (f32[256,256]{1,0:T(8,128)S(1)}, f32[256,256]{1,0:T(8,128)}, u32[]{:S(2)}) copy-start(f32[256,256]{1,0:T(8,128)} %constant.10.clone.forward) | copy-start | bytes 786436
  39.4 44.7 %copy-start.6 = (f32[256,256]{1,0:T(8,128)S(1)}, f32[256,256]{1,0:T(8,128)}, u32[]{:S(2)}) copy-start(f32[256,256]{1,0:T(8,128)} %constant.11.clone.backward) | copy-start | bytes 786436
  86.8 34.3 %all-to-all-start.3 = ((f32[64,32,128]{2,1,0:T(8,128)}), f32[64,32,128]{2,1,0:T(8,128)S(1)}, u32[]{:S(2)}, u32[]{:S(2)}) async-start(f32[64,32,128]{2,1,0:T(8,128)} %bitcast.5), calls=%async_computation.3 | async-start | bytes 2097152 | tf_op jit(solution)/shard_map/to_planes/all_to_all | solution.py:210
  93.0 13.9 %collective-permute-start.1 = (f32[4,128,128]{2,1,0:T(8,128)S(1)}, f32[4,128,128]{2,1,0:T(8,128)S(1)}, u32[]{:S(2)}, u32[]{:S(2)}) collective-permute-start(f32[4,128,128]{2,1,0:T(8,128)S(1)} %bitcast.12), channel_id=1, source_target_pairs={{0,256},{32,288},{64,320},{96,352},{128,384},{160,416},{192,448},{... | collective-permute-start | bytes 786440 | tf_op jit(solution)/shard_map/swap_received/ppermute | solution.py:198

commit v4 on v3

--- a/solution.py
+++ b/solution.py
@@ -13,6 +13,7 @@
 LANES = 128
 BATCH = 2
 RING = 8
+SHARES = 2
 VMEM_LIMIT = 40 * 1024 * 1024
 
 
@@ -43,8 +44,21 @@
     return dot(high, matrix[0]) + (dot(low, matrix[0]) + dot(high, matrix[1]))
 
 
-def spread_kernel(owner, occupied, pieces, out):
-    piece = pieces[owner[0]]
+def choice_kernel(owner, occupied, leader, weight):
+    leader[...] = jnp.broadcast_to(owner[:, :1].astype(jnp.float32), leader.shape)
+    ring = lax.axis_index("band") // RING
+    group = lax.broadcasted_iota(jnp.int32, occupied.shape, 1)
+    named = (group == owner[:, :1]) & (occupied[...] == ring)
+    count = jnp.sum(jnp.where(named, 1.0, 0.0), axis=(0, 1), keepdims=True)
+    weight[...] = jnp.broadcast_to(count, weight.shape)
+
+
+def spread_kernel(leader, pieces, out):
+    shape = pieces.shape[1:]
+    chosen = jnp.broadcast_to(leader[:1], shape)
+    piece = jnp.zeros(shape, jnp.float32)
+    for k in range(pieces.shape[0]):
+        piece = jnp.where(chosen == float(k), pieces[k], piece)
     for k in range(out.shape[0]):
         out[k] = piece
 
@@ -81,14 +95,13 @@
     return signed.astype(jnp.float32) * (2.0 * math.pi / length)
 
 
-def middle_kernel(owner, occupied, field, forward, backward, out):
+def middle_kernel(weight, field, forward, backward, out, result, done):
     sources, rows, fields, parts, lanes = field.shape
     planes = parts // 2
     length = sources * planes
     size = sources * parts
     ring = lax.axis_index("band") // RING
-    weight = sum((occupied[j, owner[0]] == ring).astype(jnp.float32) for j in range(occupied.shape[0]))
-    factor = weight * (-FRACTION * 4.0 * math.pi / float(length**3))
+    factor = weight[:1] * (-FRACTION * 4.0 * math.pi / float(length**3))
     row = lax.broadcasted_iota(jnp.int32, (size, lanes), 0)
     x_index = (row // parts) * planes + row % planes
     wave_x = signed_wave(x_index, length)
@@ -102,11 +115,22 @@
     items = [(k, s) for k in range(rows) for s in range(fields)]
     value = jnp.concatenate([field[:, k, s].reshape(size, lanes) for k, s in items], axis=1)
     value = left_product(forward, value) * jnp.concatenate(kernels, axis=1)
-    value = left_product(backward, value)
-    for n, (k, s) in enumerate(items):
-        target = ring if s == 0 else 1 - ring
-        part = value[:, n * lanes : (n + 1) * lanes]
-        out[target, :, k] = part.reshape(sources, parts, lanes)
+    copies = []
+    step = sources // SHARES
+    for share in range(SHARES):
+        part = slice(share * step, (share + 1) * step)
+        matrix = [m[share * step * parts : (share + 1) * step * parts] for m in backward]
+        solved = left_product(matrix, value)
+        for n, (k, s) in enumerate(items):
+            block = solved[:, n * lanes : (n + 1) * lanes]
+            result[s, part, k] = block.reshape(step, parts, lanes)
+        for s, target in enumerate((ring, 1 - ring)):
+            copies.append(
+                pltpu.make_async_copy(result.at[s, part], out.at[target, part], done.at[s, share])
+            )
+            copies[-1].start()
+    for copy in copies:
+        copy.wait()
 
 
 def backward_kernel(field, own, other, left, right, out, result, done):
@@ -136,19 +160,19 @@
         copy.wait()
 
 
-def smem():
-    return pl.BlockSpec(memory_space=pltpu.SMEM)
-
-
 def vmem():
     return pl.BlockSpec(memory_space=pltpu.VMEM)
+
+
+def is_shape(value):
+    return isinstance(value, tuple)
 
 
 def call(kernel, shape, specs, flops, name, **options):
     options.setdefault("out_specs", vmem())
     return pl.pallas_call(
         kernel,
-        out_shape=jax.ShapeDtypeStruct(shape, jnp.float32),
+        out_shape=jax.tree.map(lambda s: jax.ShapeDtypeStruct(s, jnp.float32), shape, is_leaf=is_shape),
         in_specs=specs,
         compiler_params=pltpu.CompilerParams(vmem_limit_bytes=VMEM_LIMIT),
         cost_estimate=pl.CostEstimate(flops=flops, bytes_accessed=4 << 20, transcendentals=0),
@@ -172,9 +196,15 @@
 
     with jax.named_scope("scatter"):
         pieces = lax.all_to_all(orbitals.reshape(groups, -1, LANES), "band", 0, 0, tiled=True)
-    mine = call(
-        spread_kernel, (ring,) + pieces.shape[1:], [smem()] * 2 + [vmem()], 0, "spread"
-    )(owner, order, pieces)
+    leader, weight = call(
+        choice_kernel,
+        [(8, LANES)] * 2,
+        [vmem()] * 2,
+        flops // 2,
+        "choice",
+        out_specs=[vmem()] * 2,
+    )(owner.reshape(1, -1), order)
+    mine = call(spread_kernel, (ring,) + pieces.shape[1:], [vmem()] * 2, 0, "spread")(leader, pieces)
     rings = [[a * ring + y for y in range(ring)] for a in range(2)]
     with jax.named_scope("gather"):
         received = lax.all_to_all(mine, "band", 0, 0, axis_index_groups=rings, tiled=True)
@@ -199,10 +229,15 @@
     spectrum = call(
         middle_kernel,
         (2, columns, rows, 2 * planes, LANES),
-        [smem()] * 2 + [vmem()] * 3,
+        [vmem()] * 4,
         flops,
         "solve_x",
-    )(owner, order, spectrum.reshape(columns, rows, 2, 2 * planes, LANES), x_forward, x_backward)
+        out_specs=pl.BlockSpec(memory_space=pl.ANY),
+        scratch_shapes=[
+            pltpu.VMEM((2, columns, rows, 2 * planes, LANES), jnp.float32),
+            pltpu.SemaphoreType.DMA((2, SHARES)),
+        ],
+    )(weight, spectrum.reshape(columns, rows, 2, 2 * planes, LANES), x_forward, x_backward)
     sharing = [
         [(a * ring + y) * columns + f for a in range(2) for f in range(columns)] for y in range(ring)
     ]

time: 124 us -> 122 us (0.984)
    pallas_call x2 -> x3, Pallas kernels: 3.97 us -> 2.9 us  [the longest x1 1.98 us: body(): call(middle_kernel, (2, columns, rows, 2 * planes, LANES), [vmem()] * 4,...]
where the time goes in v4:
time: 122 us
  blocking collectives  44.7 us (37%)
  waiting for transfers between devices  43 us (35%)
  starting transfers between devices  27 us (22%)
  Pallas kernels  6.4 us (5%)
    all_to_all x1, blocking collectives, body(): lax.all_to_all(spectrum.reshape(columns, rows * 2 * 2 * planes, LANES), '...  44.7 us
    all_to_all x1, waiting for transfers between devices, body(): lax.all_to_all(spectrum.reshape(2 * columns, rows * 2 * planes, LANES), (...  14.1 us
    ppermute x1, waiting for transfers between devices, body(): received_other = lax.ppermute(received, 'band', swap)  10.5 us
    all_to_all x1, waiting for transfers between devices, body(): lax.all_to_all(orbitals.reshape(groups, -1, LANES), 'band', 0, 0, tiled=T...  9 us
    all_to_all x1, starting transfers between devices, body(): lax.all_to_all(orbitals.reshape(groups, -1, LANES), 'band', 0, 0, tiled=T...  8.81 us
    all_to_all x1, waiting for transfers between devices, body(): lax.all_to_all(mine, 'band', 0, 0, axis_index_groups=rings, tiled=True)  8.67 us
    all_to_all x1, starting transfers between devices, body(): lax.all_to_all(spectrum.reshape(2 * columns, rows * 2 * planes, LANES), (...  6.21 us
    all_to_all x1, starting transfers between devices, body(): lax.all_to_all(mine, 'band', 0, 0, axis_index_groups=rings, tiled=True)  5.31 us
  transfers between devices with their start and end apart: 5, of which 5 were waited for; matrix products, arithmetic and copies ran while one was open for 0% of the time, Pallas kernels for 1%

profile of v4, /device:TPU:1, one launch (start us, length us, event | category | flops | bytes accessed | tf_op | source)
XLA Modules:
  0.0 121.9 jit_solution(16844815918978650111)
XLA Ops:
  0.0 0.0 copy-start
  0.0 8.8 %all-to-all-start = ((f32[16,64,128]{2,1,0:T(8,128)}), f32[16,64,128]{2,1,0:T(8,128)S(1)}, u32[]{:S(2)}, u32[]{:S(2)}) async-start(f32[16,64,128]{2,1,0:T(8,128)} %bitcast.11), calls=%async_computation | async-start | bytes 1048576 | tf_op jit(solution)/shard_map/scatter/all_to_all | solution.py:198
  8.8 0.0 copy-done
  8.8 3.3 %collective-permute-start = (f32[2,4,128,128]{3,2,1,0:T(8,128)S(1)}, f32[2,4,128,128]{3,2,1,0:T(8,128)S(1)}, u32[]{:S(2)}, u32[]{:S(2)}) collective-permute-start(f32[2,4,128,128]{3,2,1,0:T(8,128)S(1)} %copy-done), channel_id=1, source_target_pairs={{0,256},{32,288},{64,320},{96,352},{128,384},{160,416},{192,448},{... | collective-permute-start | bytes 1572872 | tf_op jit(solution)/shard_map/swap_orbitals/ppermute | solution.py:195
  12.1 0.0 copy-start.1
  12.1 0.0 copy-start.2
  12.1 0.7 copy-done.1
  12.8 0.0 copy-done.2
  12.8 0.2 choice.1
  13.0 9.0 %all-to-all-done.pieces = f32[16,64,128]{2,1,0:T(8,128)S(1)} async-done(((f32[16,64,128]{2,1,0:T(8,128)}), f32[16,64,128]{2,1,0:T(8,128)S(1)}, u32[]{:S(2)}, u32[]{:S(2)}) %all-to-all-start) | async-done | bytes 524320 | tf_op jit(solution)/shard_map/scatter/all_to_all | solution.py:198
  22.0 0.7 spread.1
  22.7 0.0 copy-start.3
  22.7 0.0 copy-start.4
  22.7 5.3 %all-to-all-start.1 = ((f32[8,64,128]{2,1,0:T(8,128)}), f32[8,64,128]{2,1,0:T(8,128)S(1)}, u32[]{:S(2)}, u32[]{:S(2)}) async-start(f32[8,64,128]{2,1,0:T(8,128)} %spread.1), calls=%async_computation.1 | async-start | bytes 524288 | tf_op jit(solution)/shard_map/gather/all_to_all | solution.py:210
  28.1 0.6 collective-permute-done.other
  28.7 8.7 %all-to-all-done.1 = f32[8,64,128]{2,1,0:T(8,128)S(1)} async-done(((f32[8,64,128]{2,1,0:T(8,128)}), f32[8,64,128]{2,1,0:T(8,128)S(1)}, u32[]{:S(2)}, u32[]{:S(2)}) %all-to-all-start.1) | async-done | bytes 262176 | tf_op jit(solution)/shard_map/gather/all_to_all | solution.py:210
  37.4 0.0 copy-done.3
  37.4 0.0 copy-done.4
  37.4 1.4 %forward_zy.1 = f32[2048,128]{1,0:T(8,128)S(1)} custom-call(f32[2,4,128,128]{3,2,1,0:T(8,128)S(1)} %copy-done, f32[2,4,128,128]{3,2,1,0:T(8,128)S(1)} %collective-permute-done.other, f32[4,128,128]{2,1,0:T(8,128)S(1)} %bitcast.12, f32[256,256]{1,0:T(8,128)S(1)} %copy-done.3, f32[256,256]{1,0:T(8,128)S(1)} %copy-done.4), custom_call_target="tpu_custom_call" | custom-call | flops 805306368 | bytes 4194304 | tf_op jit(solution)/shard_map/forward_zy/pallas_call | solution.py:220
  38.8 0.0 copy-start.5
  38.8 0.0 copy-start.6
  38.8 44.7 %all_to_all.20 = f32[32,64,128]{2,1,0:T(8,128)S(1)} all-to-all(f32[32,64,128]{2,1,0:T(8,128)S(1)} %bitcast.10), channel_id=1, replica_groups=mesh['band'=16,'fft'=32] {'fft'}, dimensions={0} | all-to-all | bytes 2097152 | tf_op jit(solution)/shard_map/to_columns/all_to_all | solution.py:224
  83.5 0.0 copy-done.5
  83.5 0.0 copy-done.6
  83.5 2.0 %solve_x.1 = f32[2,32,4,8,128]{4,3,2,1,0:T(8,128)} custom-call(f32[8,128]{1,0:T(8,128)S(1)} %get-tuple-element.7.weight, f32[32,4,2,8,128]{4,3,2,1,0:T(8,128)S(1)} %bitcast.9, f32[256,256]{1,0:T(8,128)S(1)} %copy-done.5, f32[256,256]{1,0:T(8,128)S(1)} %copy-done.6), custom_call_target="tpu_custom_call" | custom-call | flops 805306368 | bytes 4194304 | tf_op jit(solution)/shard_map/solve_x/pallas_call | solution.py:229
  85.5 6.2 %all-to-all-start.3 = ((f32[64,32,128]{2,1,0:T(8,128)}), f32[64,32,128]{2,1,0:T(8,128)S(1)}, u32[]{:S(2)}, u32[]{:S(2)}) async-start(f32[64,32,128]{2,1,0:T(8,128)} %bitcast.6), calls=%async_computation.3 | async-start | bytes 2097152 | tf_op jit(solution)/shard_map/to_planes/all_to_all | solution.py:245
  91.7 3.4 %collective-permute-start.1 = (f32[4,128,128]{2,1,0:T(8,128)S(1)}, f32[4,128,128]{2,1,0:T(8,128)S(1)}, u32[]{:S(2)}, u32[]{:S(2)}) collective-permute-start(f32[4,128,128]{2,1,0:T(8,128)S(1)} %bitcast.13), channel_id=1, source_target_pairs={{0,256},{32,288},{64,320},{96,352},{128,384},{160,416},{192,448},{... | collective-permute-start | bytes 786440 | tf_op jit(solution)/shard_map/swap_received/ppermute | solution.py:228
  95.1 10.5 %collective-permute-done.1.other = f32[4,128,128]{2,1,0:T(8,128)S(1)} collective-permute-done((f32[4,128,128]{2,1,0:T(8,128)S(1)}, f32[4,128,128]{2,1,0:T(8,128)S(1)}, u32[]{:S(2)}, u32[]{:S(2)}) %collective-permute-start.1) | collective-permute-done | bytes 262176 | tf_op jit(solution)/shard_map/swap_received/ppermute | solution.py:228
  105.7 14.1 %all-to-all-done.3 = f32[64,32,128]{2,1,0:T(8,128)S(1)} async-done(((f32[64,32,128]{2,1,0:T(8,128)}), f32[64,32,128]{2,1,0:T(8,128)S(1)}, u32[]{:S(2)}, u32[]{:S(2)}) %all-to-all-start.3) | async-done | bytes 1048608 | tf_op jit(solution)/shard_map/to_planes/all_to_all | solution.py:245
  119.8 2.1 %backward_yz.1 = f32[2,4,128,128]{3,2,1,0:T(8,128)} custom-call(f32[2,1024,128]{2,1,0:T(8,128)S(1)} %bitcast.8, f32[4,128,128]{2,1,0:T(8,128)S(1)} %bitcast.14, f32[4,128,128]{2,1,0:T(8,128)S(1)} %collective-permute-done.1.other, f32[256,256]{1,0:T(8,128)S(1)} %copy-done.4, f32[256,256]{1,0:T(8,128)S(1)} %copy-done.3), custom_call_target="tpu_custom_call" | custom-call | flops 805306368 | bytes 4194304 | tf_op jit(solution)/shard_map/backward_yz/pallas_call | solution.py:253
Async XLA Ops:
  0.0 8.8 %copy-start = (f32[2,4,128,128]{3,2,1,0:T(8,128)S(1)}, f32[2,4,128,128]{3,2,1,0:T(8,128)}, u32[]{:S(2)}) copy-start(f32[2,4,128,128]{3,2,1,0:T(8,128)} %own.1) | copy-start | bytes 1572868
  0.0 22.0 %all-to-all-start = ((f32[16,64,128]{2,1,0:T(8,128)}), f32[16,64,128]{2,1,0:T(8,128)S(1)}, u32[]{:S(2)}, u32[]{:S(2)}) async-start(f32[16,64,128]{2,1,0:T(8,128)} %bitcast.11), calls=%async_computation | async-start | bytes 1048576 | tf_op jit(solution)/shard_map/scatter/all_to_all | solution.py:198
  8.8 19.9 %collective-permute-start = (f32[2,4,128,128]{3,2,1,0:T(8,128)S(1)}, f32[2,4,128,128]{3,2,1,0:T(8,128)S(1)}, u32[]{:S(2)}, u32[]{:S(2)}) collective-permute-start(f32[2,4,128,128]{3,2,1,0:T(8,128)S(1)} %copy-done), channel_id=1, source_target_pairs={{0,256},{32,288},{64,320},{96,352},{128,384},{160,416},{192,448},{... | collective-permute-start | bytes 1572872 | tf_op jit(solution)/shard_map/swap_orbitals/ppermute | solution.py:195
  12.1 0.7 copy-start.1
  12.1 0.7 copy-start.2
  22.7 14.6 %copy-start.3 = (f32[256,256]{1,0:T(8,128)S(1)}, f32[256,256]{1,0:T(8,128)}, u32[]{:S(2)}) copy-start(f32[256,256]{1,0:T(8,128)} %constant.8.clone.left.right) | copy-start | bytes 786436
  22.7 14.6 %copy-start.4 = (f32[256,256]{1,0:T(8,128)S(1)}, f32[256,256]{1,0:T(8,128)}, u32[]{:S(2)}) copy-start(f32[256,256]{1,0:T(8,128)} %constant.9.clone.right.left) | copy-start | bytes 786436
  22.7 14.6 %all-to-all-start.1 = ((f32[8,64,128]{2,1,0:T(8,128)}), f32[8,64,128]{2,1,0:T(8,128)S(1)}, u32[]{:S(2)}, u32[]{:S(2)}) async-start(f32[8,64,128]{2,1,0:T(8,128)} %spread.1), calls=%async_computation.1 | async-start | bytes 524288 | tf_op jit(solution)/shard_map/gather/all_to_all | solution.py:210
  38.8 44.7 %copy-start.5 = (f32[256,256]{1,0:T(8,128)S(1)}, f32[256,256]{1,0:T(8,128)}, u32[]{:S(2)}) copy-start(f32[256,256]{1,0:T(8,128)} %constant.10.clone.forward) | copy-start | bytes 786436
  38.8 44.7 %copy-start.6 = (f32[256,256]{1,0:T(8,128)S(1)}, f32[256,256]{1,0:T(8,128)}, u32[]{:S(2)}) copy-start(f32[256,256]{1,0:T(8,128)} %constant.11.clone.backward) | copy-start | bytes 786436
  85.5 34.3 %all-to-all-start.3 = ((f32[64,32,128]{2,1,0:T(8,128)}), f32[64,32,128]{2,1,0:T(8,128)S(1)}, u32[]{:S(2)}, u32[]{:S(2)}) async-start(f32[64,32,128]{2,1,0:T(8,128)} %bitcast.6), calls=%async_computation.3 | async-start | bytes 2097152 | tf_op jit(solution)/shard_map/to_planes/all_to_all | solution.py:245
  91.7 13.9 %collective-permute-start.1 = (f32[4,128,128]{2,1,0:T(8,128)S(1)}, f32[4,128,128]{2,1,0:T(8,128)S(1)}, u32[]{:S(2)}, u32[]{:S(2)}) collective-permute-start(f32[4,128,128]{2,1,0:T(8,128)S(1)} %bitcast.13), channel_id=1, source_target_pairs={{0,256},{32,288},{64,320},{96,352},{128,384},{160,416},{192,448},{... | collective-permute-start | bytes 786440 | tf_op jit(solution)/shard_map/swap_received/ppermute | solution.py:228

commit v5 on v4

--- a/solution.py
+++ b/solution.py
@@ -14,6 +14,7 @@
 BATCH = 2
 RING = 8
 SHARES = 2
+PLANES = 4
 VMEM_LIMIT = 40 * 1024 * 1024
 
 
@@ -139,23 +140,28 @@
     partners = ((ring, own), (1 - ring, other))
     left, right = split(left[...]), split(right[...])
     copies = []
-    for p in range(planes):
+    for first in range(0, planes, PLANES):
+        group = range(first, first + PLANES)
         blocks = []
         for c in range(2):
-            rows = pl.ds(c * planes + p, length, stride=2 * planes)
-            blocks.append(jnp.concatenate([field[j, rows, :] for j, _ in partners], axis=1))
+            rows = [pl.ds(c * planes + p, length, stride=2 * planes) for p in group]
+            blocks.append(
+                jnp.concatenate([field[j, row, :] for row in rows for j, _ in partners], axis=1)
+            )
         along_y = left_product(left, jnp.concatenate(blocks, axis=0))
         wide = [
             jnp.concatenate([tile(along_y, c, k, length) for c in range(2)], axis=1)
-            for k in range(len(partners))
+            for k in range(PLANES * len(partners))
         ]
         both = right_product(jnp.concatenate(wide, axis=0), right)
-        for c in range(2):
-            result[c, p] = sum(
-                tile(both, k, c, length) * partner[p] for k, (_, partner) in enumerate(partners)
-            )
-            copies.append(pltpu.make_async_copy(result.at[c, p], out.at[c, p], done.at[c, p]))
-            copies[-1].start()
+        for n, p in enumerate(group):
+            for c in range(2):
+                result[c, p] = sum(
+                    tile(both, n * len(partners) + k, c, length) * partner[p]
+                    for k, (_, partner) in enumerate(partners)
+                )
+                copies.append(pltpu.make_async_copy(result.at[c, p], out.at[c, p], done.at[c, p]))
+                copies[-1].start()
     for copy in copies:
         copy.wait()
 

time: 122 us -> 122 us (level)
  no operation moved by 1% of the time
where the time goes in v5:
time: 122 us
  blocking collectives  44.7 us (37%)
  waiting for transfers between devices  43 us (35%)
  starting transfers between devices  27 us (22%)
  Pallas kernels  6.21 us (5%)
    all_to_all x1, blocking collectives, body(): lax.all_to_all(spectrum.reshape(columns, rows * 2 * 2 * planes, LANES), '...  44.7 us
    all_to_all x1, waiting for transfers between devices, body(): lax.all_to_all(spectrum.reshape(2 * columns, rows * 2 * planes, LANES), (...  14.1 us
    ppermute x1, waiting for transfers between devices, body(): received_other = lax.ppermute(received, 'band', swap)  10.5 us
    all_to_all x1, waiting for transfers between devices, body(): lax.all_to_all(orbitals.reshape(groups, -1, LANES), 'band', 0, 0, tiled=T...  9 us
    all_to_all x1, starting transfers between devices, body(): lax.all_to_all(orbitals.reshape(groups, -1, LANES), 'band', 0, 0, tiled=T...  8.81 us
    all_to_all x1, waiting for transfers between devices, body(): lax.all_to_all(mine, 'band', 0, 0, axis_index_groups=rings, tiled=True)  8.67 us
    all_to_all x1, starting transfers between devices, body(): lax.all_to_all(spectrum.reshape(2 * columns, rows * 2 * planes, LANES), (...  6.21 us
    all_to_all x1, starting transfers between devices, body(): lax.all_to_all(mine, 'band', 0, 0, axis_index_groups=rings, tiled=True)  5.31 us
  transfers between devices with their start and end apart: 5, of which 5 were waited for; matrix products, arithmetic and copies ran while one was open for 0% of the time, Pallas kernels for 1%

profile of v5, /device:TPU:1, one launch (start us, length us, event | category | flops | bytes accessed | tf_op | source)
XLA Modules:
  0.0 121.7 jit_solution(3122979540932999641)
XLA Ops:
  0.0 0.0 copy-start
  0.0 8.8 %all-to-all-start = ((f32[16,64,128]{2,1,0:T(8,128)}), f32[16,64,128]{2,1,0:T(8,128)S(1)}, u32[]{:S(2)}, u32[]{:S(2)}) async-start(f32[16,64,128]{2,1,0:T(8,128)} %bitcast.11), calls=%async_computation | async-start | bytes 1048576 | tf_op jit(solution)/shard_map/scatter/all_to_all | solution.py:204
  8.8 0.0 copy-done
  8.8 3.3 %collective-permute-start = (f32[2,4,128,128]{3,2,1,0:T(8,128)S(1)}, f32[2,4,128,128]{3,2,1,0:T(8,128)S(1)}, u32[]{:S(2)}, u32[]{:S(2)}) collective-permute-start(f32[2,4,128,128]{3,2,1,0:T(8,128)S(1)} %copy-done), channel_id=1, source_target_pairs={{0,256},{32,288},{64,320},{96,352},{128,384},{160,416},{192,448},{... | collective-permute-start | bytes 1572872 | tf_op jit(solution)/shard_map/swap_orbitals/ppermute | solution.py:201
  12.1 0.0 copy-start.1
  12.1 0.0 copy-start.2
  12.1 0.7 copy-done.1
  12.8 0.0 copy-done.2
  12.8 0.2 choice.1
  13.0 9.0 %all-to-all-done.pieces = f32[16,64,128]{2,1,0:T(8,128)S(1)} async-done(((f32[16,64,128]{2,1,0:T(8,128)}), f32[16,64,128]{2,1,0:T(8,128)S(1)}, u32[]{:S(2)}, u32[]{:S(2)}) %all-to-all-start) | async-done | bytes 524320 | tf_op jit(solution)/shard_map/scatter/all_to_all | solution.py:204
  22.0 0.7 spread.1
  22.7 0.0 copy-start.3
  22.7 0.0 copy-start.4
  22.7 5.3 %all-to-all-start.1 = ((f32[8,64,128]{2,1,0:T(8,128)}), f32[8,64,128]{2,1,0:T(8,128)S(1)}, u32[]{:S(2)}, u32[]{:S(2)}) async-start(f32[8,64,128]{2,1,0:T(8,128)} %spread.1), calls=%async_computation.1 | async-start | bytes 524288 | tf_op jit(solution)/shard_map/gather/all_to_all | solution.py:216
  28.1 0.6 collective-permute-done.other
  28.7 8.7 %all-to-all-done.1 = f32[8,64,128]{2,1,0:T(8,128)S(1)} async-done(((f32[8,64,128]{2,1,0:T(8,128)}), f32[8,64,128]{2,1,0:T(8,128)S(1)}, u32[]{:S(2)}, u32[]{:S(2)}) %all-to-all-start.1) | async-done | bytes 262176 | tf_op jit(solution)/shard_map/gather/all_to_all | solution.py:216
  37.4 0.0 copy-done.3
  37.4 0.0 copy-done.4
  37.4 1.4 %forward_zy.1 = f32[2048,128]{1,0:T(8,128)S(1)} custom-call(f32[2,4,128,128]{3,2,1,0:T(8,128)S(1)} %copy-done, f32[2,4,128,128]{3,2,1,0:T(8,128)S(1)} %collective-permute-done.other, f32[4,128,128]{2,1,0:T(8,128)S(1)} %bitcast.12, f32[256,256]{1,0:T(8,128)S(1)} %copy-done.3, f32[256,256]{1,0:T(8,128)S(1)} %copy-done.4), custom_call_target="tpu_custom_call" | custom-call | flops 805306368 | bytes 4194304 | tf_op jit(solution)/shard_map/forward_zy/pallas_call | solution.py:226
  38.8 0.0 copy-start.5
  38.8 0.0 copy-start.6
  38.8 44.7 %all_to_all.20 = f32[32,64,128]{2,1,0:T(8,128)S(1)} all-to-all(f32[32,64,128]{2,1,0:T(8,128)S(1)} %bitcast.10), channel_id=1, replica_groups=mesh['band'=16,'fft'=32] {'fft'}, dimensions={0} | all-to-all | bytes 2097152 | tf_op jit(solution)/shard_map/to_columns/all_to_all | solution.py:230
  83.5 0.0 copy-done.5
  83.5 0.0 copy-done.6
  83.5 2.0 %solve_x.1 = f32[2,32,4,8,128]{4,3,2,1,0:T(8,128)} custom-call(f32[8,128]{1,0:T(8,128)S(1)} %get-tuple-element.7.weight, f32[32,4,2,8,128]{4,3,2,1,0:T(8,128)S(1)} %bitcast.9, f32[256,256]{1,0:T(8,128)S(1)} %copy-done.5, f32[256,256]{1,0:T(8,128)S(1)} %copy-done.6), custom_call_target="tpu_custom_call" | custom-call | flops 805306368 | bytes 4194304 | tf_op jit(solution)/shard_map/solve_x/pallas_call | solution.py:235
  85.5 6.2 %all-to-all-start.3 = ((f32[64,32,128]{2,1,0:T(8,128)}), f32[64,32,128]{2,1,0:T(8,128)S(1)}, u32[]{:S(2)}, u32[]{:S(2)}) async-start(f32[64,32,128]{2,1,0:T(8,128)} %bitcast.6), calls=%async_computation.3 | async-start | bytes 2097152 | tf_op jit(solution)/shard_map/to_planes/all_to_all | solution.py:251
  91.7 3.4 %collective-permute-start.1 = (f32[4,128,128]{2,1,0:T(8,128)S(1)}, f32[4,128,128]{2,1,0:T(8,128)S(1)}, u32[]{:S(2)}, u32[]{:S(2)}) collective-permute-start(f32[4,128,128]{2,1,0:T(8,128)S(1)} %bitcast.13), channel_id=1, source_target_pairs={{0,256},{32,288},{64,320},{96,352},{128,384},{160,416},{192,448},{... | collective-permute-start | bytes 786440 | tf_op jit(solution)/shard_map/swap_received/ppermute | solution.py:234
  95.1 10.5 %collective-permute-done.1.other = f32[4,128,128]{2,1,0:T(8,128)S(1)} collective-permute-done((f32[4,128,128]{2,1,0:T(8,128)S(1)}, f32[4,128,128]{2,1,0:T(8,128)S(1)}, u32[]{:S(2)}, u32[]{:S(2)}) %collective-permute-start.1) | collective-permute-done | bytes 262176 | tf_op jit(solution)/shard_map/swap_received/ppermute | solution.py:234
  105.7 14.1 %all-to-all-done.3 = f32[64,32,128]{2,1,0:T(8,128)S(1)} async-done(((f32[64,32,128]{2,1,0:T(8,128)}), f32[64,32,128]{2,1,0:T(8,128)S(1)}, u32[]{:S(2)}, u32[]{:S(2)}) %all-to-all-start.3) | async-done | bytes 1048608 | tf_op jit(solution)/shard_map/to_planes/all_to_all | solution.py:251
  119.8 1.9 %backward_yz.1 = f32[2,4,128,128]{3,2,1,0:T(8,128)} custom-call(f32[2,1024,128]{2,1,0:T(8,128)S(1)} %bitcast.8, f32[4,128,128]{2,1,0:T(8,128)S(1)} %bitcast.14, f32[4,128,128]{2,1,0:T(8,128)S(1)} %collective-permute-done.1.other, f32[256,256]{1,0:T(8,128)S(1)} %copy-done.4, f32[256,256]{1,0:T(8,128)S(1)} %copy-done.3), custom_call_target="tpu_custom_call" | custom-call | flops 805306368 | bytes 4194304 | tf_op jit(solution)/shard_map/backward_yz/pallas_call | solution.py:259
Async XLA Ops:
  0.0 8.8 %copy-start = (f32[2,4,128,128]{3,2,1,0:T(8,128)S(1)}, f32[2,4,128,128]{3,2,1,0:T(8,128)}, u32[]{:S(2)}) copy-start(f32[2,4,128,128]{3,2,1,0:T(8,128)} %own.1) | copy-start | bytes 1572868
  0.0 22.0 %all-to-all-start = ((f32[16,64,128]{2,1,0:T(8,128)}), f32[16,64,128]{2,1,0:T(8,128)S(1)}, u32[]{:S(2)}, u32[]{:S(2)}) async-start(f32[16,64,128]{2,1,0:T(8,128)} %bitcast.11), calls=%async_computation | async-start | bytes 1048576 | tf_op jit(solution)/shard_map/scatter/all_to_all | solution.py:204
  8.8 19.9 %collective-permute-start = (f32[2,4,128,128]{3,2,1,0:T(8,128)S(1)}, f32[2,4,128,128]{3,2,1,0:T(8,128)S(1)}, u32[]{:S(2)}, u32[]{:S(2)}) collective-permute-start(f32[2,4,128,128]{3,2,1,0:T(8,128)S(1)} %copy-done), channel_id=1, source_target_pairs={{0,256},{32,288},{64,320},{96,352},{128,384},{160,416},{192,448},{... | collective-permute-start | bytes 1572872 | tf_op jit(solution)/shard_map/swap_orbitals/ppermute | solution.py:201
  12.1 0.7 copy-start.1
  12.1 0.7 copy-start.2
  22.7 14.6 %copy-start.3 = (f32[256,256]{1,0:T(8,128)S(1)}, f32[256,256]{1,0:T(8,128)}, u32[]{:S(2)}) copy-start(f32[256,256]{1,0:T(8,128)} %constant.8.clone.left.right) | copy-start | bytes 786436
  22.7 14.6 %copy-start.4 = (f32[256,256]{1,0:T(8,128)S(1)}, f32[256,256]{1,0:T(8,128)}, u32[]{:S(2)}) copy-start(f32[256,256]{1,0:T(8,128)} %constant.9.clone.right.left) | copy-start | bytes 786436
  22.7 14.6 %all-to-all-start.1 = ((f32[8,64,128]{2,1,0:T(8,128)}), f32[8,64,128]{2,1,0:T(8,128)S(1)}, u32[]{:S(2)}, u32[]{:S(2)}) async-start(f32[8,64,128]{2,1,0:T(8,128)} %spread.1), calls=%async_computation.1 | async-start | bytes 524288 | tf_op jit(solution)/shard_map/gather/all_to_all | solution.py:216
  38.8 44.7 %copy-start.5 = (f32[256,256]{1,0:T(8,128)S(1)}, f32[256,256]{1,0:T(8,128)}, u32[]{:S(2)}) copy-start(f32[256,256]{1,0:T(8,128)} %constant.10.clone.forward) | copy-start | bytes 786436
  38.8 44.7 %copy-start.6 = (f32[256,256]{1,0:T(8,128)S(1)}, f32[256,256]{1,0:T(8,128)}, u32[]{:S(2)}) copy-start(f32[256,256]{1,0:T(8,128)} %constant.11.clone.backward) | copy-start | bytes 786436
  85.5 34.3 %all-to-all-start.3 = ((f32[64,32,128]{2,1,0:T(8,128)}), f32[64,32,128]{2,1,0:T(8,128)S(1)}, u32[]{:S(2)}, u32[]{:S(2)}) async-start(f32[64,32,128]{2,1,0:T(8,128)} %bitcast.6), calls=%async_computation.3 | async-start | bytes 2097152 | tf_op jit(solution)/shard_map/to_planes/all_to_all | solution.py:251
  91.7 13.9 %collective-permute-start.1 = (f32[4,128,128]{2,1,0:T(8,128)S(1)}, f32[4,128,128]{2,1,0:T(8,128)S(1)}, u32[]{:S(2)}, u32[]{:S(2)}) collective-permute-start(f32[4,128,128]{2,1,0:T(8,128)S(1)} %bitcast.13), channel_id=1, source_target_pairs={{0,256},{32,288},{64,320},{96,352},{128,384},{160,416},{192,448},{... | collective-permute-start | bytes 786440 | tf_op jit(solution)/shard_map/swap_received/ppermute | solution.py:234

commit v6 on v5

--- a/solution.py
+++ b/solution.py
@@ -13,6 +13,7 @@
 LANES = 128
 BATCH = 2
 RING = 8
+PLACES = (0, 4, 2, 6, 1, 5, 3, 7)
 SHARES = 2
 PLANES = 4
 VMEM_LIMIT = 40 * 1024 * 1024
@@ -68,8 +69,15 @@
     return value[row * size : (row + 1) * size, column * size : (column + 1) * size]
 
 
+def plane(received, p):
+    pieces = len(PLACES) // (received.shape[0] * received.shape[1] // LANES)
+    return jnp.concatenate(
+        [received[PLACES.index(p * pieces + k)] for k in range(pieces)], axis=0
+    )
+
+
 def forward_kernel(own, other, received, left, right, out):
-    planes, length = received.shape[0], received.shape[1]
+    planes, length = own.shape[1], own.shape[2]
     stride = 2 * 2 * planes
     left, right = split(left[...]), split(right[...])
     for s, orbitals in enumerate((own, other)):
@@ -77,7 +85,7 @@
             group = range(first, first + BATCH)
             fields = []
             for p in group:
-                partner = received[p]
+                partner = plane(received, p)
                 fields.append(jnp.concatenate([orbitals[c, p] * partner for c in range(2)], axis=1))
             along_z = right_product(jnp.concatenate(fields, axis=0), right)
             blocks = [
@@ -135,7 +143,7 @@
 
 
 def backward_kernel(field, own, other, left, right, out, result, done):
-    planes, length = own.shape[0], own.shape[1]
+    planes, length = result.shape[1], result.shape[2]
     ring = lax.axis_index("band") // RING
     partners = ((ring, own), (1 - ring, other))
     left, right = split(left[...]), split(right[...])
@@ -157,7 +165,7 @@
         for n, p in enumerate(group):
             for c in range(2):
                 result[c, p] = sum(
-                    tile(both, n * len(partners) + k, c, length) * partner[p]
+                    tile(both, n * len(partners) + k, c, length) * plane(partner, p)
                     for k, (_, partner) in enumerate(partners)
                 )
                 copies.append(pltpu.make_async_copy(result.at[c, p], out.at[c, p], done.at[c, p]))
@@ -211,10 +219,9 @@
         out_specs=[vmem()] * 2,
     )(owner.reshape(1, -1), order)
     mine = call(spread_kernel, (ring,) + pieces.shape[1:], [vmem()] * 2, 0, "spread")(leader, pieces)
-    rings = [[a * ring + y for y in range(ring)] for a in range(2)]
+    rings = [[a * ring + y for y in PLACES] for a in range(2)]
     with jax.named_scope("gather"):
         received = lax.all_to_all(mine, "band", 0, 0, axis_index_groups=rings, tiled=True)
-    received = received.reshape(planes, length, length)
 
     matrix = wave_matrix(length)
     left, right = matrix, matrix.T.copy()

time: 122 us -> 120 us (0.984)
  waiting for transfers between devices: 43 us -> 40.8 us
    all_to_all x1, waiting for transfers between devices: 8.67 us -> 6.46 us  [body(): lax.all_to_all(mine, 'band', 0, 0, axis_index_groups=rings, tiled=True)]
where the time goes in v6:
time: 120 us; the launch traced here: 119 us
  blocking collectives  44.6 us (37%)
  waiting for transfers between devices  40.8 us (34%)
  starting transfers between devices  27 us (22%)
  Pallas kernels  6.21 us (5%)
    all_to_all x1, blocking collectives, body(): lax.all_to_all(spectrum.reshape(columns, rows * 2 * 2 * planes, LANES), '...  44.6 us
    all_to_all x1, waiting for transfers between devices, body(): lax.all_to_all(spectrum.reshape(2 * columns, rows * 2 * planes, LANES), (...  14.1 us
    ppermute x1, waiting for transfers between devices, body(): received_other = lax.ppermute(received, 'band', swap)  10.5 us
    all_to_all x1, waiting for transfers between devices, body(): lax.all_to_all(orbitals.reshape(groups, -1, LANES), 'band', 0, 0, tiled=T...  9 us
    all_to_all x1, starting transfers between devices, body(): lax.all_to_all(orbitals.reshape(groups, -1, LANES), 'band', 0, 0, tiled=T...  8.81 us
    all_to_all x1, waiting for transfers between devices, body(): lax.all_to_all(mine, 'band', 0, 0, axis_index_groups=rings, tiled=True)  6.46 us
    all_to_all x1, starting transfers between devices, body(): lax.all_to_all(spectrum.reshape(2 * columns, rows * 2 * planes, LANES), (...  6.21 us
    all_to_all x1, starting transfers between devices, body(): lax.all_to_all(mine, 'band', 0, 0, axis_index_groups=rings, tiled=True)  5.31 us
  transfers between devices with their start and end apart: 5, of which 5 were waited for; matrix products, arithmetic and copies ran while one was open for 0% of the time, Pallas kernels for 1%

profile of v6, /device:TPU:1, one launch (start us, length us, event | category | flops | bytes accessed | tf_op | source)
XLA Modules:
  0.0 119.3 jit_solution(8252270252202155341)
XLA Ops:
  0.0 0.0 copy-start
  0.0 8.8 %all-to-all-start = ((f32[16,64,128]{2,1,0:T(8,128)}), f32[16,64,128]{2,1,0:T(8,128)S(1)}, u32[]{:S(2)}, u32[]{:S(2)}) async-start(f32[16,64,128]{2,1,0:T(8,128)} %bitcast.10), calls=%async_computation | async-start | bytes 1048576 | tf_op jit(solution)/shard_map/scatter/all_to_all | solution.py:212
  8.8 0.0 copy-done
  8.8 3.3 %collective-permute-start = (f32[2,4,128,128]{3,2,1,0:T(8,128)S(1)}, f32[2,4,128,128]{3,2,1,0:T(8,128)S(1)}, u32[]{:S(2)}, u32[]{:S(2)}) collective-permute-start(f32[2,4,128,128]{3,2,1,0:T(8,128)S(1)} %copy-done), channel_id=1, source_target_pairs={{0,256},{32,288},{64,320},{96,352},{128,384},{160,416},{192,448},{... | collective-permute-start | bytes 1572872 | tf_op jit(solution)/shard_map/swap_orbitals/ppermute | solution.py:209
  12.1 0.0 copy-start.1
  12.1 0.0 copy-start.2
  12.1 0.7 copy-done.1
  12.8 0.0 copy-done.2
  12.8 0.2 choice.1
  13.0 9.0 %all-to-all-done.pieces = f32[16,64,128]{2,1,0:T(8,128)S(1)} async-done(((f32[16,64,128]{2,1,0:T(8,128)}), f32[16,64,128]{2,1,0:T(8,128)S(1)}, u32[]{:S(2)}, u32[]{:S(2)}) %all-to-all-start) | async-done | bytes 524320 | tf_op jit(solution)/shard_map/scatter/all_to_all | solution.py:212
  22.0 0.7 spread.1
  22.7 0.0 copy-start.3
  22.7 0.0 copy-start.4
  22.7 5.3 %all-to-all-start.1 = ((f32[8,64,128]{2,1,0:T(8,128)}), f32[8,64,128]{2,1,0:T(8,128)S(1)}, u32[]{:S(2)}, u32[]{:S(2)}) async-start(f32[8,64,128]{2,1,0:T(8,128)} %spread.1), calls=%async_computation.1 | async-start | bytes 524288 | tf_op jit(solution)/shard_map/gather/all_to_all | solution.py:224
  28.1 0.6 collective-permute-done.other
  28.7 6.5 %all-to-all-done.1.received.own = f32[8,64,128]{2,1,0:T(8,128)S(1)} async-done(((f32[8,64,128]{2,1,0:T(8,128)}), f32[8,64,128]{2,1,0:T(8,128)S(1)}, u32[]{:S(2)}, u32[]{:S(2)}) %all-to-all-start.1) | async-done | bytes 262176 | tf_op jit(solution)/shard_map/gather/all_to_all | solution.py:224
  35.2 0.0 copy-done.3
  35.2 0.0 copy-done.4
  35.2 1.4 %forward_zy.1 = f32[2048,128]{1,0:T(8,128)S(1)} custom-call(f32[2,4,128,128]{3,2,1,0:T(8,128)S(1)} %copy-done, f32[2,4,128,128]{3,2,1,0:T(8,128)S(1)} %collective-permute-done.other, f32[8,64,128]{2,1,0:T(8,128)S(1)} %all-to-all-done.1.received.own, f32[256,256]{1,0:T(8,128)S(1)} %copy-done.3, f32[256,256]{1,0:T(8,128)S(1)} %copy-done.4), custom_call_target="tpu_custom_call" | custom-call | flops 805306368 | bytes 4194304 | tf_op jit(solution)/shard_map/forward_zy/pallas_call | solution.py:233
  36.6 0.0 copy-start.5
  36.6 0.0 copy-start.6
  36.6 44.6 %all_to_all.20 = f32[32,64,128]{2,1,0:T(8,128)S(1)} all-to-all(f32[32,64,128]{2,1,0:T(8,128)S(1)} %bitcast.9), channel_id=1, replica_groups=mesh['band'=16,'fft'=32] {'fft'}, dimensions={0} | all-to-all | bytes 2097152 | tf_op jit(solution)/shard_map/to_columns/all_to_all | solution.py:237
  81.2 0.0 copy-done.5
  81.2 0.0 copy-done.6
  81.2 2.0 %solve_x.1 = f32[2,32,4,8,128]{4,3,2,1,0:T(8,128)} custom-call(f32[8,128]{1,0:T(8,128)S(1)} %get-tuple-element.7.weight, f32[32,4,2,8,128]{4,3,2,1,0:T(8,128)S(1)} %bitcast.8, f32[256,256]{1,0:T(8,128)S(1)} %copy-done.5, f32[256,256]{1,0:T(8,128)S(1)} %copy-done.6), custom_call_target="tpu_custom_call" | custom-call | flops 805306368 | bytes 4194304 | tf_op jit(solution)/shard_map/solve_x/pallas_call | solution.py:242
  83.2 6.2 %all-to-all-start.3 = ((f32[64,32,128]{2,1,0:T(8,128)}), f32[64,32,128]{2,1,0:T(8,128)S(1)}, u32[]{:S(2)}, u32[]{:S(2)}) async-start(f32[64,32,128]{2,1,0:T(8,128)} %bitcast.5), calls=%async_computation.3 | async-start | bytes 2097152 | tf_op jit(solution)/shard_map/to_planes/all_to_all | solution.py:258
  89.4 3.4 %collective-permute-start.1 = (f32[8,64,128]{2,1,0:T(8,128)S(1)}, f32[8,64,128]{2,1,0:T(8,128)S(1)}, u32[]{:S(2)}, u32[]{:S(2)}) collective-permute-start(f32[8,64,128]{2,1,0:T(8,128)S(1)} %all-to-all-done.1.received.own), channel_id=1, source_target_pairs={{0,256},{32,288},{64,320},{96,352},{128,384},{160,416},{192,448},{... | collective-permute-start | bytes 786440 | tf_op jit(solution)/shard_map/swap_received/ppermute | solution.py:241
  92.8 10.5 %collective-permute-done.1.other = f32[8,64,128]{2,1,0:T(8,128)S(1)} collective-permute-done((f32[8,64,128]{2,1,0:T(8,128)S(1)}, f32[8,64,128]{2,1,0:T(8,128)S(1)}, u32[]{:S(2)}, u32[]{:S(2)}) %collective-permute-start.1) | collective-permute-done | bytes 262176 | tf_op jit(solution)/shard_map/swap_received/ppermute | solution.py:241
  103.3 14.1 %all-to-all-done.3 = f32[64,32,128]{2,1,0:T(8,128)S(1)} async-done(((f32[64,32,128]{2,1,0:T(8,128)}), f32[64,32,128]{2,1,0:T(8,128)S(1)}, u32[]{:S(2)}, u32[]{:S(2)}) %all-to-all-start.3) | async-done | bytes 1048608 | tf_op jit(solution)/shard_map/to_planes/all_to_all | solution.py:258
  117.4 1.9 %backward_yz.1 = f32[2,4,128,128]{3,2,1,0:T(8,128)} custom-call(f32[2,1024,128]{2,1,0:T(8,128)S(1)} %bitcast.7, f32[8,64,128]{2,1,0:T(8,128)S(1)} %all-to-all-done.1.received.own, f32[8,64,128]{2,1,0:T(8,128)S(1)} %collective-permute-done.1.other, f32[256,256]{1,0:T(8,128)S(1)} %copy-done.4, f32[256,256]{1,0:T(8,128)S(1)} %copy-done.3), custom_call_target="tpu_custom_call" | custom-call | flops 805306368 | bytes 4194304 | tf_op jit(solution)/shard_map/backward_yz/pallas_call | solution.py:266
Async XLA Ops:
  0.0 8.8 %copy-start = (f32[2,4,128,128]{3,2,1,0:T(8,128)S(1)}, f32[2,4,128,128]{3,2,1,0:T(8,128)}, u32[]{:S(2)}) copy-start(f32[2,4,128,128]{3,2,1,0:T(8,128)} %own.1) | copy-start | bytes 1572868
  0.0 22.0 %all-to-all-start = ((f32[16,64,128]{2,1,0:T(8,128)}), f32[16,64,128]{2,1,0:T(8,128)S(1)}, u32[]{:S(2)}, u32[]{:S(2)}) async-start(f32[16,64,128]{2,1,0:T(8,128)} %bitcast.10), calls=%async_computation | async-start | bytes 1048576 | tf_op jit(solution)/shard_map/scatter/all_to_all | solution.py:212
  8.8 19.9 %collective-permute-start = (f32[2,4,128,128]{3,2,1,0:T(8,128)S(1)}, f32[2,4,128,128]{3,2,1,0:T(8,128)S(1)}, u32[]{:S(2)}, u32[]{:S(2)}) collective-permute-start(f32[2,4,128,128]{3,2,1,0:T(8,128)S(1)} %copy-done), channel_id=1, source_target_pairs={{0,256},{32,288},{64,320},{96,352},{128,384},{160,416},{192,448},{... | collective-permute-start | bytes 1572872 | tf_op jit(solution)/shard_map/swap_orbitals/ppermute | solution.py:209
  12.1 0.7 copy-start.1
  12.1 0.7 copy-start.2
  22.7 12.4 %copy-start.3 = (f32[256,256]{1,0:T(8,128)S(1)}, f32[256,256]{1,0:T(8,128)}, u32[]{:S(2)}) copy-start(f32[256,256]{1,0:T(8,128)} %constant.8.clone.left.right) | copy-start | bytes 786436
  22.7 12.4 %copy-start.4 = (f32[256,256]{1,0:T(8,128)S(1)}, f32[256,256]{1,0:T(8,128)}, u32[]{:S(2)}) copy-start(f32[256,256]{1,0:T(8,128)} %constant.9.clone.right.left) | copy-start | bytes 786436
  22.7 12.4 %all-to-all-start.1 = ((f32[8,64,128]{2,1,0:T(8,128)}), f32[8,64,128]{2,1,0:T(8,128)S(1)}, u32[]{:S(2)}, u32[]{:S(2)}) async-start(f32[8,64,128]{2,1,0:T(8,128)} %spread.1), calls=%async_computation.1 | async-start | bytes 524288 | tf_op jit(solution)/shard_map/gather/all_to_all | solution.py:224
  36.6 44.6 %copy-start.5 = (f32[256,256]{1,0:T(8,128)S(1)}, f32[256,256]{1,0:T(8,128)}, u32[]{:S(2)}) copy-start(f32[256,256]{1,0:T(8,128)} %constant.10.clone.forward) | copy-start | bytes 786436
  36.6 44.6 %copy-start.6 = (f32[256,256]{1,0:T(8,128)S(1)}, f32[256,256]{1,0:T(8,128)}, u32[]{:S(2)}) copy-start(f32[256,256]{1,0:T(8,128)} %constant.11.clone.backward) | copy-start | bytes 786436
  83.2 34.3 %all-to-all-start.3 = ((f32[64,32,128]{2,1,0:T(8,128)}), f32[64,32,128]{2,1,0:T(8,128)S(1)}, u32[]{:S(2)}, u32[]{:S(2)}) async-start(f32[64,32,128]{2,1,0:T(8,128)} %bitcast.5), calls=%async_computation.3 | async-start | bytes 2097152 | tf_op jit(solution)/shard_map/to_planes/all_to_all | solution.py:258
  89.4 13.9 %collective-permute-start.1 = (f32[8,64,128]{2,1,0:T(8,128)S(1)}, f32[8,64,128]{2,1,0:T(8,128)S(1)}, u32[]{:S(2)}, u32[]{:S(2)}) collective-permute-start(f32[8,64,128]{2,1,0:T(8,128)S(1)} %all-to-all-done.1.received.own), channel_id=1, source_target_pairs={{0,256},{32,288},{64,320},{96,352},{128,384},{160,416},{192,448},{... | collective-permute-start | bytes 786440 | tf_op jit(solution)/shard_map/swap_received/ppermute | solution.py:241

commit v7 on v6

--- a/solution.py
+++ b/solution.py
@@ -16,6 +16,7 @@
 PLACES = (0, 4, 2, 6, 1, 5, 3, 7)
 SHARES = 2
 PLANES = 4
+MATRICES = 4
 VMEM_LIMIT = 40 * 1024 * 1024
 
 
@@ -46,13 +47,26 @@
     return dot(high, matrix[0]) + (dot(low, matrix[0]) + dot(high, matrix[1]))
 
 
-def choice_kernel(owner, occupied, leader, weight):
+def prepare_kernel(owner, occupied, *refs):
+    matrices, (leader, *parts, table) = refs[:MATRICES], refs[MATRICES:]
     leader[...] = jnp.broadcast_to(owner[:, :1].astype(jnp.float32), leader.shape)
+    for matrix, part in zip(matrices, parts):
+        part[0], part[1] = split(matrix[...])
     ring = lax.axis_index("band") // RING
     group = lax.broadcasted_iota(jnp.int32, occupied.shape, 1)
     named = (group == owner[:, :1]) & (occupied[...] == ring)
     count = jnp.sum(jnp.where(named, 1.0, 0.0), axis=(0, 1), keepdims=True)
-    weight[...] = jnp.broadcast_to(count, weight.shape)
+    rows, size, lanes = table.shape
+    length = size // 2
+    planes = length // lax.axis_size("fft")
+    row = lax.broadcasted_iota(jnp.int32, (size, lanes), 0)
+    wave_x = signed_wave((row // (2 * planes)) * planes + row % planes, length)
+    wave_z = signed_wave(lax.broadcasted_iota(jnp.int32, (size, lanes), 1), length)
+    flat = wave_x * wave_x + wave_z * wave_z + SCREEN
+    factor = count * (-FRACTION * 4.0 * math.pi / float(length**3))
+    for k in range(rows):
+        wave_y = signed_wave(lax.axis_index("fft") * rows + k, length)
+        table[k] = factor / (flat + wave_y * wave_y)
 
 
 def spread_kernel(leader, pieces, out):
@@ -79,7 +93,6 @@
 def forward_kernel(own, other, received, left, right, out):
     planes, length = own.shape[1], own.shape[2]
     stride = 2 * 2 * planes
-    left, right = split(left[...]), split(right[...])
     for s, orbitals in enumerate((own, other)):
         for first in range(0, planes, BATCH):
             group = range(first, first + BATCH)
@@ -104,31 +117,19 @@
     return signed.astype(jnp.float32) * (2.0 * math.pi / length)
 
 
-def middle_kernel(weight, field, forward, backward, out, result, done):
+def middle_kernel(table, field, forward, backward, out, result, done):
     sources, rows, fields, parts, lanes = field.shape
-    planes = parts // 2
-    length = sources * planes
     size = sources * parts
     ring = lax.axis_index("band") // RING
-    factor = weight[:1] * (-FRACTION * 4.0 * math.pi / float(length**3))
-    row = lax.broadcasted_iota(jnp.int32, (size, lanes), 0)
-    x_index = (row // parts) * planes + row % planes
-    wave_x = signed_wave(x_index, length)
-    wave_z = signed_wave(lax.broadcasted_iota(jnp.int32, (size, lanes), 1), length)
-    flat = wave_x * wave_x + wave_z * wave_z + SCREEN
-    forward, backward = split(forward[...]), split(backward[...])
-    kernels = []
-    for k in range(rows):
-        wave_y = signed_wave(lax.axis_index("fft") * rows + k, length)
-        kernels += [factor / (flat + wave_y * wave_y)] * fields
     items = [(k, s) for k in range(rows) for s in range(fields)]
     value = jnp.concatenate([field[:, k, s].reshape(size, lanes) for k, s in items], axis=1)
-    value = left_product(forward, value) * jnp.concatenate(kernels, axis=1)
+    kernels = jnp.concatenate([table[k] for k, _ in items], axis=1)
+    value = left_product(forward, value) * kernels
     copies = []
     step = sources // SHARES
     for share in range(SHARES):
         part = slice(share * step, (share + 1) * step)
-        matrix = [m[share * step * parts : (share + 1) * step * parts] for m in backward]
+        matrix = [backward[h, share * step * parts : (share + 1) * step * parts] for h in range(2)]
         solved = left_product(matrix, value)
         for n, (k, s) in enumerate(items):
             block = solved[:, n * lanes : (n + 1) * lanes]
@@ -146,7 +147,6 @@
     planes, length = result.shape[1], result.shape[2]
     ring = lax.axis_index("band") // RING
     partners = ((ring, own), (1 - ring, other))
-    left, right = split(left[...]), split(right[...])
     copies = []
     for first in range(0, planes, PLANES):
         group = range(first, first + PLANES)
@@ -178,15 +178,15 @@
     return pl.BlockSpec(memory_space=pltpu.VMEM)
 
 
-def is_shape(value):
-    return isinstance(value, tuple)
-
-
-def call(kernel, shape, specs, flops, name, **options):
+def call(kernel, shape, specs, flops, name, types=jnp.float32, **options):
     options.setdefault("out_specs", vmem())
+    if isinstance(shape, list):
+        out_shape = [jax.ShapeDtypeStruct(s, t) for s, t in zip(shape, types)]
+    else:
+        out_shape = jax.ShapeDtypeStruct(shape, types)
     return pl.pallas_call(
         kernel,
-        out_shape=jax.tree.map(lambda s: jax.ShapeDtypeStruct(s, jnp.float32), shape, is_leaf=is_shape),
+        out_shape=out_shape,
         in_specs=specs,
         compiler_params=pltpu.CompilerParams(vmem_limit_bytes=VMEM_LIMIT),
         cost_estimate=pl.CostEstimate(flops=flops, bytes_accessed=4 << 20, transcendentals=0),
@@ -210,25 +210,23 @@
 
     with jax.named_scope("scatter"):
         pieces = lax.all_to_all(orbitals.reshape(groups, -1, LANES), "band", 0, 0, tiled=True)
-    leader, weight = call(
-        choice_kernel,
-        [(8, LANES)] * 2,
-        [vmem()] * 2,
-        flops // 2,
-        "choice",
-        out_specs=[vmem()] * 2,
-    )(owner.reshape(1, -1), order)
+    matrix = wave_matrix(length)
+    x_index = np.arange(length).reshape(columns, 1, planes) + np.array([0, length])[None, :, None]
+    x_index = x_index.reshape(-1)
+    mixed = matrix[np.ix_(x_index, x_index)]
+    leader, left, right, x_forward, x_backward, table = call(
+        prepare_kernel,
+        [(8, LANES)] + [(2, 2 * length, 2 * length)] * MATRICES + [(rows, 2 * length, LANES)],
+        [vmem()] * (2 + MATRICES),
+        flops,
+        "prepare",
+        types=[jnp.float32] + [jnp.bfloat16] * MATRICES + [jnp.float32],
+        out_specs=[vmem()] * (2 + MATRICES),
+    )(owner.reshape(1, -1), order, matrix, matrix.T.copy(), mixed, mixed.T.copy())
     mine = call(spread_kernel, (ring,) + pieces.shape[1:], [vmem()] * 2, 0, "spread")(leader, pieces)
     rings = [[a * ring + y for y in PLACES] for a in range(2)]
     with jax.named_scope("gather"):
         received = lax.all_to_all(mine, "band", 0, 0, axis_index_groups=rings, tiled=True)
-
-    matrix = wave_matrix(length)
-    left, right = matrix, matrix.T.copy()
-    x_index = np.arange(length).reshape(columns, 1, planes) + np.array([0, length])[None, :, None]
-    x_index = x_index.reshape(-1)
-    mixed = matrix[np.ix_(x_index, x_index)]
-    x_forward, x_backward = mixed, mixed.T.copy()
 
     spectrum = call(
         forward_kernel, (length * 2 * 2 * planes, LANES), [vmem()] * 5, flops, "forward_zy"
@@ -250,7 +248,7 @@
             pltpu.VMEM((2, columns, rows, 2 * planes, LANES), jnp.float32),
             pltpu.SemaphoreType.DMA((2, SHARES)),
         ],
-    )(weight, spectrum.reshape(columns, rows, 2, 2 * planes, LANES), x_forward, x_backward)
+    )(table, spectrum.reshape(columns, rows, 2, 2 * planes, LANES), x_forward, x_backward)
     sharing = [
         [(a * ring + y) * columns + f for a in range(2) for f in range(columns)] for y in range(ring)
     ]

time: 120 us -> 120 us (level)
  waiting for transfers between devices: 40.8 us -> 37.2 us
  local copies, waits for them, and re-layouts: 0.69 us -> 3.94 us
    all_to_all x1, waiting for transfers between devices: 9 us -> 5.48 us  [body(): lax.all_to_all(orbitals.reshape(groups, -1, LANES), 'band', 0, 0, tiled=T...]
    unnamed x14 -> x22, local copies, waits for them, and re-layouts: 0.69 us -> 3.94 us
where the time goes in v7:
time: 120 us; the launch traced here: 119 us
  blocking collectives  44.4 us (37%)
  waiting for transfers between devices  37.2 us (31%)
  starting transfers between devices  27 us (22%)
  Pallas kernels  6.37 us (5%)
  local copies, waits for them, and re-layouts  3.94 us (3%)
    all_to_all x1, blocking collectives, body(): lax.all_to_all(spectrum.reshape(columns, rows * 2 * 2 * planes, LANES), '...  44.4 us
    all_to_all x1, waiting for transfers between devices, body(): lax.all_to_all(spectrum.reshape(2 * columns, rows * 2 * planes, LANES), (...  14.1 us
    ppermute x1, waiting for transfers between devices, body(): received_other = lax.ppermute(received, 'band', swap)  10.5 us
    all_to_all x1, starting transfers between devices, body(): lax.all_to_all(orbitals.reshape(groups, -1, LANES), 'band', 0, 0, tiled=T...  8.83 us
    all_to_all x1, waiting for transfers between devices, body(): lax.all_to_all(mine, 'band', 0, 0, axis_index_groups=rings, tiled=True)  6.45 us
    all_to_all x1, starting transfers between devices, body(): lax.all_to_all(spectrum.reshape(2 * columns, rows * 2 * planes, LANES), (...  6.2 us
    all_to_all x1, waiting for transfers between devices, body(): lax.all_to_all(orbitals.reshape(groups, -1, LANES), 'band', 0, 0, tiled=T...  5.48 us
    all_to_all x1, starting transfers between devices, body(): lax.all_to_all(mine, 'band', 0, 0, axis_index_groups=rings, tiled=True)  5.33 us
  transfers between devices with their start and end apart: 5, of which 5 were waited for; matrix products, arithmetic and copies ran while one was open for 0% of the time, Pallas kernels for 1%

profile of v7, /device:TPU:1, one launch (start us, length us, event | category | flops | bytes accessed | tf_op | source)
XLA Modules:
  0.0 119.1 jit_solution(14633085254214535385)
XLA Ops:
  0.0 0.0 copy-start
  0.0 0.0 copy-start.3
  0.0 8.8 %all-to-all-start = ((f32[16,64,128]{2,1,0:T(8,128)}), f32[16,64,128]{2,1,0:T(8,128)S(1)}, u32[]{:S(2)}, u32[]{:S(2)}) async-start(f32[16,64,128]{2,1,0:T(8,128)} %bitcast.10), calls=%async_computation | async-start | bytes 1048576 | tf_op jit(solution)/shard_map/scatter/all_to_all | solution.py:212
  8.8 0.0 copy-done
  8.9 3.3 %collective-permute-start = (f32[2,4,128,128]{3,2,1,0:T(8,128)S(1)}, f32[2,4,128,128]{3,2,1,0:T(8,128)S(1)}, u32[]{:S(2)}, u32[]{:S(2)}) collective-permute-start(f32[2,4,128,128]{3,2,1,0:T(8,128)S(1)} %copy-done), channel_id=1, source_target_pairs={{0,256},{32,288},{64,320},{96,352},{128,384},{160,416},{192,448},{... | collective-permute-start | bytes 1572872 | tf_op jit(solution)/shard_map/swap_orbitals/ppermute | solution.py:209
  12.1 0.0 copy-start.1
  12.1 0.0 copy-start.2
  12.2 0.0 copy-done.3
  12.2 0.0 copy-done.4
  12.2 0.6 copy-done.1
  12.8 0.0 copy-done.2
  12.8 0.9 copy-done.5
  13.8 0.9 copy-done.6
  14.7 0.4 prepare.1
  15.1 0.0 copy-start.7
  15.2 0.7 copy-done.7
  15.8 0.7 copy-done.9
  16.5 5.5 %all-to-all-done.pieces = f32[16,64,128]{2,1,0:T(8,128)S(1)} async-done(((f32[16,64,128]{2,1,0:T(8,128)}), f32[16,64,128]{2,1,0:T(8,128)S(1)}, u32[]{:S(2)}, u32[]{:S(2)}) %all-to-all-start) | async-done | bytes 524320 | tf_op jit(solution)/shard_map/scatter/all_to_all | solution.py:212
  22.0 0.7 spread.1
  22.7 5.3 %all-to-all-start.1 = ((f32[8,64,128]{2,1,0:T(8,128)}), f32[8,64,128]{2,1,0:T(8,128)S(1)}, u32[]{:S(2)}, u32[]{:S(2)}) async-start(f32[8,64,128]{2,1,0:T(8,128)} %spread.1), calls=%async_computation.1 | async-start | bytes 524288 | tf_op jit(solution)/shard_map/gather/all_to_all | solution.py:229
  28.1 0.7 collective-permute-done.other
  28.7 6.5 %all-to-all-done.1.received.own = f32[8,64,128]{2,1,0:T(8,128)S(1)} async-done(((f32[8,64,128]{2,1,0:T(8,128)}), f32[8,64,128]{2,1,0:T(8,128)S(1)}, u32[]{:S(2)}, u32[]{:S(2)}) %all-to-all-start.1) | async-done | bytes 262176 | tf_op jit(solution)/shard_map/gather/all_to_all | solution.py:229
  35.2 0.0 copy-done.8
  35.2 0.0 copy-done.10
  35.2 1.4 %forward_zy.1 = f32[2048,128]{1,0:T(8,128)S(1)} custom-call(f32[2,4,128,128]{3,2,1,0:T(8,128)S(1)} %copy-done, f32[2,4,128,128]{3,2,1,0:T(8,128)S(1)} %collective-permute-done.other, f32[8,64,128]{2,1,0:T(8,128)S(1)} %all-to-all-done.1.received.own, bf16[2,256,256]{2,1,0:T(8,128)(2,1)S(1)} %copy-done.8, bf16[2,256,256]{2,1,0:T(8,128)(2,1)S(1)} %copy-done.10), custom_call_target="tpu_custom_call" | custom-call | flops 805306368 | bytes 4194304 | tf_op jit(solution)/shard_map/forward_zy/pallas_call | solution.py:231
  36.6 44.4 %all_to_all.20 = f32[32,64,128]{2,1,0:T(8,128)S(1)} all-to-all(f32[32,64,128]{2,1,0:T(8,128)S(1)} %bitcast.9), channel_id=1, replica_groups=mesh['band'=16,'fft'=32] {'fft'}, dimensions={0} | all-to-all | bytes 2097152 | tf_op jit(solution)/shard_map/to_columns/all_to_all | solution.py:235
  81.0 2.0 %solve_x.1 = f32[2,32,4,8,128]{4,3,2,1,0:T(8,128)} custom-call(f32[4,256,128]{2,1,0:T(8,128)S(1)} %get-tuple-element.11.table, f32[32,4,2,8,128]{4,3,2,1,0:T(8,128)S(1)} %bitcast.7, bf16[2,256,256]{2,1,0:T(8,128)(2,1)S(1)} %get-tuple-element.15.forward, bf16[2,256,256]{2,1,0:T(8,128)(2,1)S(1)} %get-tuple-element.16.backward), custom_call_target="tpu_custom_call" | custom-call | flops 805306368 | bytes 4194304 | tf_op jit(solution)/shard_map/solve_x/pallas_call | solution.py:240
  83.0 6.2 %all-to-all-start.3 = ((f32[64,32,128]{2,1,0:T(8,128)}), f32[64,32,128]{2,1,0:T(8,128)S(1)}, u32[]{:S(2)}, u32[]{:S(2)}) async-start(f32[64,32,128]{2,1,0:T(8,128)} %bitcast.5), calls=%async_computation.3 | async-start | bytes 2097152 | tf_op jit(solution)/shard_map/to_planes/all_to_all | solution.py:256
  89.2 3.4 %collective-permute-start.1 = (f32[8,64,128]{2,1,0:T(8,128)S(1)}, f32[8,64,128]{2,1,0:T(8,128)S(1)}, u32[]{:S(2)}, u32[]{:S(2)}) collective-permute-start(f32[8,64,128]{2,1,0:T(8,128)S(1)} %all-to-all-done.1.received.own), channel_id=1, source_target_pairs={{0,256},{32,288},{64,320},{96,352},{128,384},{160,416},{192,448},{... | collective-permute-start | bytes 786440 | tf_op jit(solution)/shard_map/swap_received/ppermute | solution.py:239
  92.6 10.5 %collective-permute-done.1.other = f32[8,64,128]{2,1,0:T(8,128)S(1)} collective-permute-done((f32[8,64,128]{2,1,0:T(8,128)S(1)}, f32[8,64,128]{2,1,0:T(8,128)S(1)}, u32[]{:S(2)}, u32[]{:S(2)}) %collective-permute-start.1) | collective-permute-done | bytes 262176 | tf_op jit(solution)/shard_map/swap_received/ppermute | solution.py:239
  103.1 14.1 %all-to-all-done.3 = f32[64,32,128]{2,1,0:T(8,128)S(1)} async-done(((f32[64,32,128]{2,1,0:T(8,128)}), f32[64,32,128]{2,1,0:T(8,128)S(1)}, u32[]{:S(2)}, u32[]{:S(2)}) %all-to-all-start.3) | async-done | bytes 1048608 | tf_op jit(solution)/shard_map/to_planes/all_to_all | solution.py:256
  117.3 1.9 %backward_yz.1 = f32[2,4,128,128]{3,2,1,0:T(8,128)} custom-call(f32[2,1024,128]{2,1,0:T(8,128)S(1)} %bitcast.8, f32[8,64,128]{2,1,0:T(8,128)S(1)} %all-to-all-done.1.received.own, f32[8,64,128]{2,1,0:T(8,128)S(1)} %collective-permute-done.1.other, bf16[2,256,256]{2,1,0:T(8,128)(2,1)S(1)} %copy-done.10, bf16[2,256,256]{2,1,0:T(8,128)(2,1)S(1)} %copy-done.8), custom_call_target="tpu_custom_call" | custom-call | flops 805306368 | bytes 4194304 | tf_op jit(solution)/shard_map/backward_yz/pallas_call | solution.py:264
  (6 shorter events, 0.0 us)
Async XLA Ops:
  0.0 8.8 %copy-start = (f32[2,4,128,128]{3,2,1,0:T(8,128)S(1)}, f32[2,4,128,128]{3,2,1,0:T(8,128)}, u32[]{:S(2)}) copy-start(f32[2,4,128,128]{3,2,1,0:T(8,128)} %own.1) | copy-start | bytes 1572868
  0.0 12.2 %copy-start.3 = (f32[256,256]{1,0:T(8,128)S(1)}, f32[256,256]{1,0:T(8,128)}, u32[]{:S(2)}) copy-start(f32[256,256]{1,0:T(8,128)} %constant.10.clone.refs_2_) | copy-start | bytes 786436
  0.0 12.2 %copy-start.4 = (f32[256,256]{1,0:T(8,128)S(1)}, f32[256,256]{1,0:T(8,128)}, u32[]{:S(2)}) copy-start(f32[256,256]{1,0:T(8,128)} %constant.11.clone.refs_3_) | copy-start | bytes 786436
  0.0 22.0 %all-to-all-start = ((f32[16,64,128]{2,1,0:T(8,128)}), f32[16,64,128]{2,1,0:T(8,128)S(1)}, u32[]{:S(2)}, u32[]{:S(2)}) async-start(f32[16,64,128]{2,1,0:T(8,128)} %bitcast.10), calls=%async_computation | async-start | bytes 1048576 | tf_op jit(solution)/shard_map/scatter/all_to_all | solution.py:212
  8.9 19.9 %collective-permute-start = (f32[2,4,128,128]{3,2,1,0:T(8,128)S(1)}, f32[2,4,128,128]{3,2,1,0:T(8,128)S(1)}, u32[]{:S(2)}, u32[]{:S(2)}) collective-permute-start(f32[2,4,128,128]{3,2,1,0:T(8,128)S(1)} %copy-done), channel_id=1, source_target_pairs={{0,256},{32,288},{64,320},{96,352},{128,384},{160,416},{192,448},{... | collective-permute-start | bytes 1572872 | tf_op jit(solution)/shard_map/swap_orbitals/ppermute | solution.py:209
  12.1 0.7 copy-start.1
  12.1 0.7 copy-start.2
  12.8 1.0 copy-start.5
  13.8 0.9 copy-start.6
  15.1 0.7 copy-start.7
  15.8 0.7 copy-start.9
  22.7 12.4 %copy-start.8 = (bf16[2,256,256]{2,1,0:T(8,128)(2,1)S(1)}, bf16[2,256,256]{2,1,0:T(8,128)(2,1)}, u32[]{:S(2)}) copy-start(bf16[2,256,256]{2,1,0:T(8,128)(2,1)} %copy-done.7) | copy-start | bytes 786436
  22.7 12.4 %copy-start.10 = (bf16[2,256,256]{2,1,0:T(8,128)(2,1)S(1)}, bf16[2,256,256]{2,1,0:T(8,128)(2,1)}, u32[]{:S(2)}) copy-start(bf16[2,256,256]{2,1,0:T(8,128)(2,1)} %copy-done.9) | copy-start | bytes 786436
  22.7 12.4 %all-to-all-start.1 = ((f32[8,64,128]{2,1,0:T(8,128)}), f32[8,64,128]{2,1,0:T(8,128)S(1)}, u32[]{:S(2)}, u32[]{:S(2)}) async-start(f32[8,64,128]{2,1,0:T(8,128)} %spread.1), calls=%async_computation.1 | async-start | bytes 524288 | tf_op jit(solution)/shard_map/gather/all_to_all | solution.py:229
  83.0 34.3 %all-to-all-start.3 = ((f32[64,32,128]{2,1,0:T(8,128)}), f32[64,32,128]{2,1,0:T(8,128)S(1)}, u32[]{:S(2)}, u32[]{:S(2)}) async-start(f32[64,32,128]{2,1,0:T(8,128)} %bitcast.5), calls=%async_computation.3 | async-start | bytes 2097152 | tf_op jit(solution)/shard_map/to_planes/all_to_all | solution.py:256
  89.2 13.9 %collective-permute-start.1 = (f32[8,64,128]{2,1,0:T(8,128)S(1)}, f32[8,64,128]{2,1,0:T(8,128)S(1)}, u32[]{:S(2)}, u32[]{:S(2)}) collective-permute-start(f32[8,64,128]{2,1,0:T(8,128)S(1)} %all-to-all-done.1.received.own), channel_id=1, source_target_pairs={{0,256},{32,288},{64,320},{96,352},{128,384},{160,416},{192,448},{... | collective-permute-start | bytes 786440 | tf_op jit(solution)/shard_map/swap_received/ppermute | solution.py:239

commit v8 on v7

--- a/solution.py
+++ b/solution.py
@@ -14,7 +14,6 @@
 BATCH = 2
 RING = 8
 PLACES = (0, 4, 2, 6, 1, 5, 3, 7)
-SHARES = 2
 PLANES = 4
 MATRICES = 4
 VMEM_LIMIT = 40 * 1024 * 1024
@@ -90,9 +89,10 @@
     )
 
 
-def forward_kernel(own, other, received, left, right, out):
+def forward_kernel(own, other, received, left, right, out, result, done):
     planes, length = own.shape[1], own.shape[2]
-    stride = 2 * 2 * planes
+    columns, _, rows, lanes = out.shape
+    copies = []
     for s, orbitals in enumerate((own, other)):
         for first in range(0, planes, BATCH):
             group = range(first, first + BATCH)
@@ -108,8 +108,13 @@
             both = left_product(left, jnp.concatenate(blocks, axis=0))
             for k, p in enumerate(group):
                 for c in range(2):
-                    row = (s * 2 + c) * planes + p
-                    out[pl.ds(row, length, stride=stride), :] = tile(both, c, k, length)
+                    place = pl.ds(c * planes + p, length, stride=2 * planes)
+                    result[s, place, :] = tile(both, c, k, length)
+        field = result.at[s].reshape(columns, rows, lanes)
+        copies.append(pltpu.make_async_copy(field, out.at[:, s], done.at[s]))
+        copies[-1].start()
+    for copy in copies:
+        copy.wait()
 
 
 def signed_wave(index, length):
@@ -117,30 +122,18 @@
     return signed.astype(jnp.float32) * (2.0 * math.pi / length)
 
 
-def middle_kernel(table, field, forward, backward, out, result, done):
-    sources, rows, fields, parts, lanes = field.shape
+def middle_kernel(table, field, forward, backward, received, out):
+    sources, fields, rows, parts, lanes = field.shape
     size = sources * parts
     ring = lax.axis_index("band") // RING
     items = [(k, s) for k in range(rows) for s in range(fields)]
-    value = jnp.concatenate([field[:, k, s].reshape(size, lanes) for k, s in items], axis=1)
+    value = jnp.concatenate([field[:, s, k].reshape(size, lanes) for k, s in items], axis=1)
     kernels = jnp.concatenate([table[k] for k, _ in items], axis=1)
-    value = left_product(forward, value) * kernels
-    copies = []
-    step = sources // SHARES
-    for share in range(SHARES):
-        part = slice(share * step, (share + 1) * step)
-        matrix = [backward[h, share * step * parts : (share + 1) * step * parts] for h in range(2)]
-        solved = left_product(matrix, value)
-        for n, (k, s) in enumerate(items):
-            block = solved[:, n * lanes : (n + 1) * lanes]
-            result[s, part, k] = block.reshape(step, parts, lanes)
-        for s, target in enumerate((ring, 1 - ring)):
-            copies.append(
-                pltpu.make_async_copy(result.at[s, part], out.at[target, part], done.at[s, share])
-            )
-            copies[-1].start()
-    for copy in copies:
-        copy.wait()
+    value = left_product(backward, left_product(forward, value) * kernels)
+    for n, (k, s) in enumerate(items):
+        target = ring if s == 0 else 1 - ring
+        block = value[:, n * lanes : (n + 1) * lanes]
+        out[target, :, k] = block.reshape(sources, parts, lanes)
 
 
 def backward_kernel(field, own, other, left, right, out, result, done):
@@ -228,8 +221,18 @@
     with jax.named_scope("gather"):
         received = lax.all_to_all(mine, "band", 0, 0, axis_index_groups=rings, tiled=True)
 
+    shape = (columns, 2, rows * 2 * planes, LANES)
     spectrum = call(
-        forward_kernel, (length * 2 * 2 * planes, LANES), [vmem()] * 5, flops, "forward_zy"
+        forward_kernel,
+        shape,
+        [vmem()] * 5,
+        flops,
+        "forward_zy",
+        out_specs=pl.BlockSpec(memory_space=pl.ANY),
+        scratch_shapes=[
+            pltpu.VMEM((2, length * 2 * planes, LANES), jnp.float32),
+            pltpu.SemaphoreType.DMA((2,)),
+        ],
     )(orbitals, other, received, left, right)
     with jax.named_scope("to_columns"):
         spectrum = lax.all_to_all(
@@ -240,15 +243,16 @@
     spectrum = call(
         middle_kernel,
         (2, columns, rows, 2 * planes, LANES),
-        [vmem()] * 4,
+        [vmem()] * 4 + [pl.BlockSpec(memory_space=pl.ANY)],
         flops,
         "solve_x",
-        out_specs=pl.BlockSpec(memory_space=pl.ANY),
-        scratch_shapes=[
-            pltpu.VMEM((2, columns, rows, 2 * planes, LANES), jnp.float32),
-            pltpu.SemaphoreType.DMA((2, SHARES)),
-        ],
-    )(table, spectrum.reshape(columns, rows, 2, 2 * planes, LANES), x_forward, x_backward)
+    )(
+        table,
+        spectrum.reshape(columns, 2, rows, 2 * planes, LANES),
+        x_forward,
+        x_backward,
+        received_other,
+    )
     sharing = [
         [(a * ring + y) * columns + f for a in range(2) for f in range(columns)] for y in range(ring)
     ]

time: 120 us -> 120 us (level)
  blocking collectives: 44.4 us -> 34.1 us
  starting transfers between devices: 27 us -> 36 us
  waiting for transfers between devices: 37.2 us -> 38.6 us
    all_to_all x1, blocking collectives: 44.4 us -> 34.1 us  [body(): lax.all_to_all(spectrum.reshape(2 * columns, rows * 2 * planes, LANES), (...]
    all_to_all x1, starting transfers between devices: 6.2 us -> 16.5 us  [body(): lax.all_to_all(spectrum.reshape(columns, rows * 2 * 2 * planes, LANES), '...]
    ppermute x1, waiting for transfers between devices: 10.5 us -> 12.3 us  [body(): received_other = lax.ppermute(received, 'band', swap)]
    ppermute x1, starting transfers between devices: 3.39 us -> 2.11 us  [body(): received_other = lax.ppermute(received, 'band', swap)]
where the time goes in v8:
time: 120 us; the launch traced here: 119 us
  waiting for transfers between devices  38.6 us (32%)
  starting transfers between devices  36 us (30%)
  blocking collectives  34.1 us (28%)
  Pallas kernels  6.27 us (5%)
  local copies, waits for them, and re-layouts  3.94 us (3%)
    all_to_all x1, blocking collectives, body(): lax.all_to_all(spectrum.reshape(2 * columns, rows * 2 * planes, LANES), (...  34.1 us
    all_to_all x1, starting transfers between devices, body(): lax.all_to_all(spectrum.reshape(columns, rows * 2 * 2 * planes, LANES), '...  16.5 us
    all_to_all x1, waiting for transfers between devices, body(): lax.all_to_all(spectrum.reshape(columns, rows * 2 * 2 * planes, LANES), '...  13.7 us
    ppermute x1, waiting for transfers between devices, body(): received_other = lax.ppermute(received, 'band', swap)  12.3 us
    all_to_all x1, starting transfers between devices, body(): lax.all_to_all(orbitals.reshape(groups, -1, LANES), 'band', 0, 0, tiled=T...  8.83 us
    all_to_all x1, waiting for transfers between devices, body(): lax.all_to_all(mine, 'band', 0, 0, axis_index_groups=rings, tiled=True)  6.45 us
    all_to_all x1, waiting for transfers between devices, body(): lax.all_to_all(orbitals.reshape(groups, -1, LANES), 'band', 0, 0, tiled=T...  5.48 us
    all_to_all x1, starting transfers between devices, body(): lax.all_to_all(mine, 'band', 0, 0, axis_index_groups=rings, tiled=True)  5.33 us
  transfers between devices with their start and end apart: 5, of which 5 were waited for; matrix products, arithmetic and copies ran while one was open for 0% of the time, Pallas kernels for 1%

profile of v8, /device:TPU:1, one launch (start us, length us, event | category | flops | bytes accessed | tf_op | source)
XLA Modules:
  0.0 119.0 jit_solution(4321933733092080386)
XLA Ops:
  0.0 0.0 copy-start
  0.0 0.0 copy-start.3
  0.0 8.8 %all-to-all-start = ((f32[16,64,128]{2,1,0:T(8,128)}), f32[16,64,128]{2,1,0:T(8,128)S(1)}, u32[]{:S(2)}, u32[]{:S(2)}) async-start(f32[16,64,128]{2,1,0:T(8,128)} %bitcast.10), calls=%async_computation | async-start | bytes 1048576 | tf_op jit(solution)/shard_map/scatter/all_to_all | solution.py:205
  8.8 0.0 copy-done
  8.9 3.3 %collective-permute-start = (f32[2,4,128,128]{3,2,1,0:T(8,128)S(1)}, f32[2,4,128,128]{3,2,1,0:T(8,128)S(1)}, u32[]{:S(2)}, u32[]{:S(2)}) collective-permute-start(f32[2,4,128,128]{3,2,1,0:T(8,128)S(1)} %copy-done), channel_id=1, source_target_pairs={{0,256},{32,288},{64,320},{96,352},{128,384},{160,416},{192,448},{... | collective-permute-start | bytes 1572872 | tf_op jit(solution)/shard_map/swap_orbitals/ppermute | solution.py:202
  12.1 0.0 copy-start.1
  12.1 0.0 copy-start.2
  12.2 0.0 copy-done.3
  12.2 0.0 copy-done.4
  12.2 0.6 copy-done.1
  12.8 0.0 copy-done.2
  12.8 0.9 copy-done.5
  13.8 0.9 copy-done.6
  14.7 0.4 prepare.1
  15.1 0.0 copy-start.7
  15.2 0.7 copy-done.7
  15.8 0.7 copy-done.9
  16.5 5.5 %all-to-all-done.pieces = f32[16,64,128]{2,1,0:T(8,128)S(1)} async-done(((f32[16,64,128]{2,1,0:T(8,128)}), f32[16,64,128]{2,1,0:T(8,128)S(1)}, u32[]{:S(2)}, u32[]{:S(2)}) %all-to-all-start) | async-done | bytes 524320 | tf_op jit(solution)/shard_map/scatter/all_to_all | solution.py:205
  22.0 0.7 spread.1
  22.7 5.3 %all-to-all-start.1 = ((f32[8,64,128]{2,1,0:T(8,128)}), f32[8,64,128]{2,1,0:T(8,128)S(1)}, u32[]{:S(2)}, u32[]{:S(2)}) async-start(f32[8,64,128]{2,1,0:T(8,128)} %spread.1), calls=%async_computation.1 | async-start | bytes 524288 | tf_op jit(solution)/shard_map/gather/all_to_all | solution.py:222
  28.1 0.7 collective-permute-done.other
  28.7 6.5 %all-to-all-done.1.received.own = f32[8,64,128]{2,1,0:T(8,128)S(1)} async-done(((f32[8,64,128]{2,1,0:T(8,128)}), f32[8,64,128]{2,1,0:T(8,128)S(1)}, u32[]{:S(2)}, u32[]{:S(2)}) %all-to-all-start.1) | async-done | bytes 262176 | tf_op jit(solution)/shard_map/gather/all_to_all | solution.py:222
  35.2 0.0 copy-done.8
  35.2 0.0 copy-done.10
  35.2 2.1 %forward_zy.1 = f32[32,2,32,128]{3,2,1,0:T(8,128)} custom-call(f32[2,4,128,128]{3,2,1,0:T(8,128)S(1)} %copy-done, f32[2,4,128,128]{3,2,1,0:T(8,128)S(1)} %collective-permute-done.other, f32[8,64,128]{2,1,0:T(8,128)S(1)} %all-to-all-done.1.received.own, bf16[2,256,256]{2,1,0:T(8,128)(2,1)S(1)} %copy-done.8, bf16[2,256,256]{2,1,0:T(8,128)(2,1)S(1)} %copy-done.10), custom_call_target="tpu_custom_call" | custom-call | flops 805306368 | bytes 4194304 | tf_op jit(solution)/shard_map/forward_zy/pallas_call | solution.py:225
  37.3 16.5 %all-to-all-start.2 = ((f32[32,64,128]{2,1,0:T(8,128)}), f32[32,64,128]{2,1,0:T(8,128)S(1)}, u32[]{:S(2)}, u32[]{:S(2)}) async-start(f32[32,64,128]{2,1,0:T(8,128)} %bitcast.3), calls=%async_computation.2 | async-start | bytes 2097152 | tf_op jit(solution)/shard_map/to_columns/all_to_all | solution.py:238
  53.8 2.1 %collective-permute-start.1 = (f32[8,64,128]{2,1,0:T(8,128)S(1)}, f32[8,64,128]{2,1,0:T(8,128)S(1)}, u32[]{:S(2)}, u32[]{:S(2)}) collective-permute-start(f32[8,64,128]{2,1,0:T(8,128)S(1)} %all-to-all-done.1.received.own), channel_id=1, source_target_pairs={{0,256},{32,288},{64,320},{96,352},{128,384},{160,416},{192,448},{... | collective-permute-start | bytes 786440 | tf_op jit(solution)/shard_map/swap_received/ppermute | solution.py:242
  55.9 12.3 %collective-permute-done.1.received.other = f32[8,64,128]{2,1,0:T(8,128)S(1)} collective-permute-done((f32[8,64,128]{2,1,0:T(8,128)S(1)}, f32[8,64,128]{2,1,0:T(8,128)S(1)}, u32[]{:S(2)}, u32[]{:S(2)}) %collective-permute-start.1) | collective-permute-done | bytes 262176 | tf_op jit(solution)/shard_map/swap_received/ppermute | solution.py:242
  68.3 13.7 %all-to-all-done.2 = f32[32,64,128]{2,1,0:T(8,128)S(1)} async-done(((f32[32,64,128]{2,1,0:T(8,128)}), f32[32,64,128]{2,1,0:T(8,128)S(1)}, u32[]{:S(2)}, u32[]{:S(2)}) %all-to-all-start.2) | async-done | bytes 1048608 | tf_op jit(solution)/shard_map/to_columns/all_to_all | solution.py:238
  82.0 1.1 solve_x.1
  83.1 34.1 %all_to_all.20 = f32[64,32,128]{2,1,0:T(8,128)S(1)} all-to-all(f32[64,32,128]{2,1,0:T(8,128)S(1)} %bitcast.8), channel_id=1, replica_groups={{0,1,2,3,4,5,6,7,8,9,10,11,12,13,14,15,16,17,18,19,20,21,22,23,24,25,26..., dimensions={0} | all-to-all | bytes 2097152 | tf_op jit(solution)/shard_map/to_planes/all_to_all | solution.py:260
  117.2 1.9 %backward_yz.1 = f32[2,4,128,128]{3,2,1,0:T(8,128)} custom-call(f32[2,1024,128]{2,1,0:T(8,128)S(1)} %bitcast.9, f32[8,64,128]{2,1,0:T(8,128)S(1)} %all-to-all-done.1.received.own, f32[8,64,128]{2,1,0:T(8,128)S(1)} %collective-permute-done.1.received.other, bf16[2,256,256]{2,1,0:T(8,128)(2,1)S(1)} %copy-done.10, bf16[2,256,256]{2,1,0:T(8,128)(2,1)S(1)} %copy-done.8), custom_call_target="tpu_custom_call" | custom-call | flops 805306368 | bytes 4194304 | tf_op jit(solution)/shard_map/backward_yz/pallas_call | solution.py:268
  (6 shorter events, 0.0 us)
Async XLA Ops:
  0.0 8.8 %copy-start = (f32[2,4,128,128]{3,2,1,0:T(8,128)S(1)}, f32[2,4,128,128]{3,2,1,0:T(8,128)}, u32[]{:S(2)}) copy-start(f32[2,4,128,128]{3,2,1,0:T(8,128)} %own.1) | copy-start | bytes 1572868
  0.0 12.2 %copy-start.3 = (f32[256,256]{1,0:T(8,128)S(1)}, f32[256,256]{1,0:T(8,128)}, u32[]{:S(2)}) copy-start(f32[256,256]{1,0:T(8,128)} %constant.10.clone.refs_2_) | copy-start | bytes 786436
  0.0 12.2 %copy-start.4 = (f32[256,256]{1,0:T(8,128)S(1)}, f32[256,256]{1,0:T(8,128)}, u32[]{:S(2)}) copy-start(f32[256,256]{1,0:T(8,128)} %constant.11.clone.refs_3_) | copy-start | bytes 786436
  0.0 22.0 %all-to-all-start = ((f32[16,64,128]{2,1,0:T(8,128)}), f32[16,64,128]{2,1,0:T(8,128)S(1)}, u32[]{:S(2)}, u32[]{:S(2)}) async-start(f32[16,64,128]{2,1,0:T(8,128)} %bitcast.10), calls=%async_computation | async-start | bytes 1048576 | tf_op jit(solution)/shard_map/scatter/all_to_all | solution.py:205
  8.9 19.9 %collective-permute-start = (f32[2,4,128,128]{3,2,1,0:T(8,128)S(1)}, f32[2,4,128,128]{3,2,1,0:T(8,128)S(1)}, u32[]{:S(2)}, u32[]{:S(2)}) collective-permute-start(f32[2,4,128,128]{3,2,1,0:T(8,128)S(1)} %copy-done), channel_id=1, source_target_pairs={{0,256},{32,288},{64,320},{96,352},{128,384},{160,416},{192,448},{... | collective-permute-start | bytes 1572872 | tf_op jit(solution)/shard_map/swap_orbitals/ppermute | solution.py:202
  12.1 0.7 copy-start.1
  12.1 0.7 copy-start.2
  12.8 1.0 copy-start.5
  13.8 0.9 copy-start.6
  15.1 0.7 copy-start.7
  15.8 0.7 copy-start.9
  22.7 12.4 %copy-start.8 = (bf16[2,256,256]{2,1,0:T(8,128)(2,1)S(1)}, bf16[2,256,256]{2,1,0:T(8,128)(2,1)}, u32[]{:S(2)}) copy-start(bf16[2,256,256]{2,1,0:T(8,128)(2,1)} %copy-done.7) | copy-start | bytes 786436
  22.7 12.4 %copy-start.10 = (bf16[2,256,256]{2,1,0:T(8,128)(2,1)S(1)}, bf16[2,256,256]{2,1,0:T(8,128)(2,1)}, u32[]{:S(2)}) copy-start(bf16[2,256,256]{2,1,0:T(8,128)(2,1)} %copy-done.9) | copy-start | bytes 786436
  22.7 12.4 %all-to-all-start.1 = ((f32[8,64,128]{2,1,0:T(8,128)}), f32[8,64,128]{2,1,0:T(8,128)S(1)}, u32[]{:S(2)}, u32[]{:S(2)}) async-start(f32[8,64,128]{2,1,0:T(8,128)} %spread.1), calls=%async_computation.1 | async-start | bytes 524288 | tf_op jit(solution)/shard_map/gather/all_to_all | solution.py:222
  37.3 44.7 %all-to-all-start.2 = ((f32[32,64,128]{2,1,0:T(8,128)}), f32[32,64,128]{2,1,0:T(8,128)S(1)}, u32[]{:S(2)}, u32[]{:S(2)}) async-start(f32[32,64,128]{2,1,0:T(8,128)} %bitcast.3), calls=%async_computation.2 | async-start | bytes 2097152 | tf_op jit(solution)/shard_map/to_columns/all_to_all | solution.py:238
  53.8 14.4 %collective-permute-start.1 = (f32[8,64,128]{2,1,0:T(8,128)S(1)}, f32[8,64,128]{2,1,0:T(8,128)S(1)}, u32[]{:S(2)}, u32[]{:S(2)}) collective-permute-start(f32[8,64,128]{2,1,0:T(8,128)S(1)} %all-to-all-done.1.received.own), channel_id=1, source_target_pairs={{0,256},{32,288},{64,320},{96,352},{128,384},{160,416},{192,448},{... | collective-permute-start | bytes 786440 | tf_op jit(solution)/shard_map/swap_received/ppermute | solution.py:242

commit v9 on v8

--- a/solution.py
+++ b/solution.py
@@ -13,7 +13,7 @@
 LANES = 128
 BATCH = 2
 RING = 8
-PLACES = (0, 4, 2, 6, 1, 5, 3, 7)
+PLACES = (0, 4, 2, 6, 3, 7, 1, 5)
 PLANES = 4
 MATRICES = 4
 VMEM_LIMIT = 40 * 1024 * 1024

time: 120 us -> 120 us (level)
  no operation moved by 1% of the time
where the time goes in v9:
time: 120 us; the launch traced here: 119 us
  waiting for transfers between devices  38.5 us (32%)
  starting transfers between devices  36.3 us (30%)
  blocking collectives  34.1 us (28%)
  Pallas kernels  6.27 us (5%)
  local copies, waits for them, and re-layouts  3.94 us (3%)
    all_to_all x1, blocking collectives, body(): lax.all_to_all(spectrum.reshape(2 * columns, rows * 2 * planes, LANES), (...  34.1 us
    all_to_all x1, starting transfers between devices, body(): lax.all_to_all(spectrum.reshape(columns, rows * 2 * 2 * planes, LANES), '...  16.6 us
    all_to_all x1, waiting for transfers between devices, body(): lax.all_to_all(spectrum.reshape(columns, rows * 2 * 2 * planes, LANES), '...  13.4 us
    ppermute x1, waiting for transfers between devices, body(): received_other = lax.ppermute(received, 'band', swap)  12.3 us
    all_to_all x1, starting transfers between devices, body(): lax.all_to_all(orbitals.reshape(groups, -1, LANES), 'band', 0, 0, tiled=T...  8.83 us
    all_to_all x1, waiting for transfers between devices, body(): lax.all_to_all(mine, 'band', 0, 0, axis_index_groups=rings, tiled=True)  6.59 us
    all_to_all x1, waiting for transfers between devices, body(): lax.all_to_all(orbitals.reshape(groups, -1, LANES), 'band', 0, 0, tiled=T...  5.48 us
    all_to_all x1, starting transfers between devices, body(): lax.all_to_all(mine, 'band', 0, 0, axis_index_groups=rings, tiled=True)  5.33 us
  transfers between devices with their start and end apart: 5, of which 5 were waited for; matrix products, arithmetic and copies ran while one was open for 0% of the time, Pallas kernels for 1%

profile of v9, /device:TPU:1, one launch (start us, length us, event | category | flops | bytes accessed | tf_op | source)
XLA Modules:
  0.0 119.2 jit_solution(416118963536456084)
XLA Ops:
  0.0 0.0 copy-start
  0.0 0.0 copy-start.3
  0.0 8.8 %all-to-all-start = ((f32[16,64,128]{2,1,0:T(8,128)}), f32[16,64,128]{2,1,0:T(8,128)S(1)}, u32[]{:S(2)}, u32[]{:S(2)}) async-start(f32[16,64,128]{2,1,0:T(8,128)} %bitcast.10), calls=%async_computation | async-start | bytes 1048576 | tf_op jit(solution)/shard_map/scatter/all_to_all | solution.py:205
  8.8 0.0 copy-done
  8.9 3.3 %collective-permute-start = (f32[2,4,128,128]{3,2,1,0:T(8,128)S(1)}, f32[2,4,128,128]{3,2,1,0:T(8,128)S(1)}, u32[]{:S(2)}, u32[]{:S(2)}) collective-permute-start(f32[2,4,128,128]{3,2,1,0:T(8,128)S(1)} %copy-done), channel_id=1, source_target_pairs={{0,256},{32,288},{64,320},{96,352},{128,384},{160,416},{192,448},{... | collective-permute-start | bytes 1572872 | tf_op jit(solution)/shard_map/swap_orbitals/ppermute | solution.py:202
  12.1 0.0 copy-start.1
  12.1 0.0 copy-start.2
  12.2 0.0 copy-done.3
  12.2 0.0 copy-done.4
  12.2 0.6 copy-done.1
  12.8 0.0 copy-done.2
  12.8 0.9 copy-done.5
  13.8 0.9 copy-done.6
  14.7 0.4 prepare.1
  15.1 0.0 copy-start.7
  15.2 0.7 copy-done.7
  15.8 0.7 copy-done.9
  16.5 5.5 %all-to-all-done.pieces = f32[16,64,128]{2,1,0:T(8,128)S(1)} async-done(((f32[16,64,128]{2,1,0:T(8,128)}), f32[16,64,128]{2,1,0:T(8,128)S(1)}, u32[]{:S(2)}, u32[]{:S(2)}) %all-to-all-start) | async-done | bytes 524320 | tf_op jit(solution)/shard_map/scatter/all_to_all | solution.py:205
  22.0 0.7 spread.1
  22.7 5.3 %all-to-all-start.1 = ((f32[8,64,128]{2,1,0:T(8,128)}), f32[8,64,128]{2,1,0:T(8,128)S(1)}, u32[]{:S(2)}, u32[]{:S(2)}) async-start(f32[8,64,128]{2,1,0:T(8,128)} %spread.1), calls=%async_computation.1 | async-start | bytes 524288 | tf_op jit(solution)/shard_map/gather/all_to_all | solution.py:222
  28.1 0.7 collective-permute-done.other
  28.7 6.6 %all-to-all-done.1.received.own = f32[8,64,128]{2,1,0:T(8,128)S(1)} async-done(((f32[8,64,128]{2,1,0:T(8,128)}), f32[8,64,128]{2,1,0:T(8,128)S(1)}, u32[]{:S(2)}, u32[]{:S(2)}) %all-to-all-start.1) | async-done | bytes 262176 | tf_op jit(solution)/shard_map/gather/all_to_all | solution.py:222
  35.3 0.0 copy-done.8
  35.3 0.0 copy-done.10
  35.3 2.1 %forward_zy.1 = f32[32,2,32,128]{3,2,1,0:T(8,128)} custom-call(f32[2,4,128,128]{3,2,1,0:T(8,128)S(1)} %copy-done, f32[2,4,128,128]{3,2,1,0:T(8,128)S(1)} %collective-permute-done.other, f32[8,64,128]{2,1,0:T(8,128)S(1)} %all-to-all-done.1.received.own, bf16[2,256,256]{2,1,0:T(8,128)(2,1)S(1)} %copy-done.8, bf16[2,256,256]{2,1,0:T(8,128)(2,1)S(1)} %copy-done.10), custom_call_target="tpu_custom_call" | custom-call | flops 805306368 | bytes 4194304 | tf_op jit(solution)/shard_map/forward_zy/pallas_call | solution.py:225
  37.4 16.6 %all-to-all-start.2 = ((f32[32,64,128]{2,1,0:T(8,128)}), f32[32,64,128]{2,1,0:T(8,128)S(1)}, u32[]{:S(2)}, u32[]{:S(2)}) async-start(f32[32,64,128]{2,1,0:T(8,128)} %bitcast.3), calls=%async_computation.2 | async-start | bytes 2097152 | tf_op jit(solution)/shard_map/to_columns/all_to_all | solution.py:238
  54.0 2.3 %collective-permute-start.1 = (f32[8,64,128]{2,1,0:T(8,128)S(1)}, f32[8,64,128]{2,1,0:T(8,128)S(1)}, u32[]{:S(2)}, u32[]{:S(2)}) collective-permute-start(f32[8,64,128]{2,1,0:T(8,128)S(1)} %all-to-all-done.1.received.own), channel_id=1, source_target_pairs={{0,256},{32,288},{64,320},{96,352},{128,384},{160,416},{192,448},{... | collective-permute-start | bytes 786440 | tf_op jit(solution)/shard_map/swap_received/ppermute | solution.py:242
  56.4 12.3 %collective-permute-done.1.received.other = f32[8,64,128]{2,1,0:T(8,128)S(1)} collective-permute-done((f32[8,64,128]{2,1,0:T(8,128)S(1)}, f32[8,64,128]{2,1,0:T(8,128)S(1)}, u32[]{:S(2)}, u32[]{:S(2)}) %collective-permute-start.1) | collective-permute-done | bytes 262176 | tf_op jit(solution)/shard_map/swap_received/ppermute | solution.py:242
  68.7 13.4 %all-to-all-done.2 = f32[32,64,128]{2,1,0:T(8,128)S(1)} async-done(((f32[32,64,128]{2,1,0:T(8,128)}), f32[32,64,128]{2,1,0:T(8,128)S(1)}, u32[]{:S(2)}, u32[]{:S(2)}) %all-to-all-start.2) | async-done | bytes 1048608 | tf_op jit(solution)/shard_map/to_columns/all_to_all | solution.py:238
  82.2 1.1 solve_x.1
  83.3 34.1 %all_to_all.20 = f32[64,32,128]{2,1,0:T(8,128)S(1)} all-to-all(f32[64,32,128]{2,1,0:T(8,128)S(1)} %bitcast.8), channel_id=1, replica_groups={{0,1,2,3,4,5,6,7,8,9,10,11,12,13,14,15,16,17,18,19,20,21,22,23,24,25,26..., dimensions={0} | all-to-all | bytes 2097152 | tf_op jit(solution)/shard_map/to_planes/all_to_all | solution.py:260
  117.4 1.9 %backward_yz.1 = f32[2,4,128,128]{3,2,1,0:T(8,128)} custom-call(f32[2,1024,128]{2,1,0:T(8,128)S(1)} %bitcast.9, f32[8,64,128]{2,1,0:T(8,128)S(1)} %all-to-all-done.1.received.own, f32[8,64,128]{2,1,0:T(8,128)S(1)} %collective-permute-done.1.received.other, bf16[2,256,256]{2,1,0:T(8,128)(2,1)S(1)} %copy-done.10, bf16[2,256,256]{2,1,0:T(8,128)(2,1)S(1)} %copy-done.8), custom_call_target="tpu_custom_call" | custom-call | flops 805306368 | bytes 4194304 | tf_op jit(solution)/shard_map/backward_yz/pallas_call | solution.py:268
  (6 shorter events, 0.0 us)
Async XLA Ops:
  0.0 8.8 %copy-start = (f32[2,4,128,128]{3,2,1,0:T(8,128)S(1)}, f32[2,4,128,128]{3,2,1,0:T(8,128)}, u32[]{:S(2)}) copy-start(f32[2,4,128,128]{3,2,1,0:T(8,128)} %own.1) | copy-start | bytes 1572868
  0.0 12.2 %copy-start.3 = (f32[256,256]{1,0:T(8,128)S(1)}, f32[256,256]{1,0:T(8,128)}, u32[]{:S(2)}) copy-start(f32[256,256]{1,0:T(8,128)} %constant.10.clone.refs_2_) | copy-start | bytes 786436
  0.0 12.2 %copy-start.4 = (f32[256,256]{1,0:T(8,128)S(1)}, f32[256,256]{1,0:T(8,128)}, u32[]{:S(2)}) copy-start(f32[256,256]{1,0:T(8,128)} %constant.11.clone.refs_3_) | copy-start | bytes 786436
  0.0 22.0 %all-to-all-start = ((f32[16,64,128]{2,1,0:T(8,128)}), f32[16,64,128]{2,1,0:T(8,128)S(1)}, u32[]{:S(2)}, u32[]{:S(2)}) async-start(f32[16,64,128]{2,1,0:T(8,128)} %bitcast.10), calls=%async_computation | async-start | bytes 1048576 | tf_op jit(solution)/shard_map/scatter/all_to_all | solution.py:205
  8.9 19.9 %collective-permute-start = (f32[2,4,128,128]{3,2,1,0:T(8,128)S(1)}, f32[2,4,128,128]{3,2,1,0:T(8,128)S(1)}, u32[]{:S(2)}, u32[]{:S(2)}) collective-permute-start(f32[2,4,128,128]{3,2,1,0:T(8,128)S(1)} %copy-done), channel_id=1, source_target_pairs={{0,256},{32,288},{64,320},{96,352},{128,384},{160,416},{192,448},{... | collective-permute-start | bytes 1572872 | tf_op jit(solution)/shard_map/swap_orbitals/ppermute | solution.py:202
  12.1 0.7 copy-start.1
  12.1 0.7 copy-start.2
  12.8 1.0 copy-start.5
  13.8 0.9 copy-start.6
  15.1 0.7 copy-start.7
  15.8 0.7 copy-start.9
  22.7 12.6 %copy-start.8 = (bf16[2,256,256]{2,1,0:T(8,128)(2,1)S(1)}, bf16[2,256,256]{2,1,0:T(8,128)(2,1)}, u32[]{:S(2)}) copy-start(bf16[2,256,256]{2,1,0:T(8,128)(2,1)} %copy-done.7) | copy-start | bytes 786436
  22.7 12.6 %copy-start.10 = (bf16[2,256,256]{2,1,0:T(8,128)(2,1)S(1)}, bf16[2,256,256]{2,1,0:T(8,128)(2,1)}, u32[]{:S(2)}) copy-start(bf16[2,256,256]{2,1,0:T(8,128)(2,1)} %copy-done.9) | copy-start | bytes 786436
  22.7 12.6 %all-to-all-start.1 = ((f32[8,64,128]{2,1,0:T(8,128)}), f32[8,64,128]{2,1,0:T(8,128)S(1)}, u32[]{:S(2)}, u32[]{:S(2)}) async-start(f32[8,64,128]{2,1,0:T(8,128)} %spread.1), calls=%async_computation.1 | async-start | bytes 524288 | tf_op jit(solution)/shard_map/gather/all_to_all | solution.py:222
  37.4 44.7 %all-to-all-start.2 = ((f32[32,64,128]{2,1,0:T(8,128)}), f32[32,64,128]{2,1,0:T(8,128)S(1)}, u32[]{:S(2)}, u32[]{:S(2)}) async-start(f32[32,64,128]{2,1,0:T(8,128)} %bitcast.3), calls=%async_computation.2 | async-start | bytes 2097152 | tf_op jit(solution)/shard_map/to_columns/all_to_all | solution.py:238
  54.0 14.7 %collective-permute-start.1 = (f32[8,64,128]{2,1,0:T(8,128)S(1)}, f32[8,64,128]{2,1,0:T(8,128)S(1)}, u32[]{:S(2)}, u32[]{:S(2)}) collective-permute-start(f32[8,64,128]{2,1,0:T(8,128)S(1)} %all-to-all-done.1.received.own), channel_id=1, source_target_pairs={{0,256},{32,288},{64,320},{96,352},{128,384},{160,416},{192,448},{... | collective-permute-start | bytes 786440 | tf_op jit(solution)/shard_map/swap_received/ppermute | solution.py:242
